TPU v7x, 128 devices: a whole 4x4x4 slice. The times are simulated.
128 devices in a mesh: sub: 32 (over x, y, core), grp: 4 (over z).
Axes of the slice: x: 4, y: 4, z: 4, core: 2. Of those that a mesh axis runs over, the one named last changes fastest.
Arguments:
- resid: bfloat16 [1024, 384, 256], P(('sub', 'grp')), may hold values from -6 to 6
- local_inv: bfloat16 [1024, 256, 256], P(('sub', 'grp')), may hold values from -0.375 to 0.375
- basis: bfloat16 [1024, 256, 128], P(('sub', 'grp')), may hold values from -0.375 to 0.375
- coarse_inv: bfloat16 [32768, 256], P(('sub', 'grp')), may hold values from -0.375 to 0.375
- coarse_map: int32 [1024, 128], P(('sub', 'grp')), may hold values from 0 to 32767, as said below
- row_counts: int32 [1024], P(('sub', 'grp')), may hold values from 64 to 128
Outputs:
- correction: float32 [1024, 384, 256], P(('sub', 'grp'))
Inputs may be any that keep to these rules, and one draw needn't show every extreme that they name: `coarse_map`: coarse degree of freedom c belongs to owner c // 256. The slots of one device's 8 subdomains name coarse degrees of freedom of any one owner at most 16 times, and every device reaches 16 for some owner.
All inputs are finite; a program needn't handle non-finite values.
Results may differ from a plain program's by a relative error of at most 0.012.
Values may be sent and summed in bfloat16 or wider, within the bound.
No kernel may reach another device: no remote copies, remote signals or barrier semaphores. Data moves between devices by JAX's collectives and lax.ppermute only.
A program may use at most 128 MiB of HBM per device.

v0:
```python
import jax
import jax.numpy as jnp
from jax import lax
from jax.sharding import PartitionSpec as P


def per_device(resid, local_inv, basis, coarse_inv, coarse_map, row_counts):
    subs, rcols, width = resid.shape
    slots_per = basis.shape[2]
    cblock = coarse_inv.shape[1]
    nsub = lax.axis_size("sub")
    ngrp = lax.axis_size("grp")
    owners = nsub * ngrp
    slots = subs * slots_per
    cap = 2 * (slots // owners)
    live = (jnp.arange(slots_per, dtype=jnp.int32)[None, :] < row_counts[:, None]).astype(
        jnp.float32
    )
    restricted = (
        jnp.einsum("smk,srm->skr", basis, resid, preferred_element_type=jnp.float32)
        * live[:, :, None]
    )
    flat_vals = restricted.reshape(slots, rcols)
    flat_ids = coarse_map.reshape(slots)
    target = flat_ids // cblock
    within = flat_ids % cblock
    order = jnp.argsort(target, stable=True)
    sorted_target = target[order]
    per_owner = jnp.sum(
        (target[:, None] == jnp.arange(owners, dtype=jnp.int32)[None, :]).astype(jnp.int32), axis=0
    )
    offsets = jnp.cumsum(per_owner) - per_owner
    position = jnp.arange(slots, dtype=jnp.int32) - offsets[sorted_target]
    slot_index = sorted_target * cap + position
    send_vals = jnp.zeros((owners * cap, rcols), jnp.float32).at[slot_index].set(flat_vals[order])
    send_ids = jnp.full((owners * cap,), cblock, jnp.int32).at[slot_index].set(within[order])
    recv_vals, recv_ids = (
        lax.all_to_all(
            send_vals.reshape(owners, cap, rcols),
            ("sub", "grp"),
            split_axis=0,
            concat_axis=0,
            tiled=True,
        ),
        lax.all_to_all(
            send_ids.reshape(owners, cap), ("sub", "grp"), split_axis=0, concat_axis=0, tiled=True
        ),
    )
    recv_vals = recv_vals.reshape(owners * cap, rcols)
    recv_ids = recv_ids.reshape(owners * cap)
    matches = (recv_ids[:, None] == jnp.arange(cblock, dtype=jnp.int32)[None, :]).astype(
        jnp.bfloat16
    )
    high_part = recv_vals.astype(jnp.bfloat16)
    low_part = (recv_vals - high_part.astype(jnp.float32)).astype(jnp.bfloat16)
    contract = (((0,), (0,)), ((), ()))
    coarse_res = lax.dot_general(matches, high_part, contract, preferred_element_type=jnp.float32)
    coarse_res = coarse_res + lax.dot_general(
        matches, low_part, contract, preferred_element_type=jnp.float32
    )
    coarse_in = coarse_res.astype(jnp.bfloat16)
    coarse_sol = jnp.dot(coarse_inv, coarse_in, preferred_element_type=jnp.float32).astype(
        jnp.bfloat16
    )
    whole = lax.all_gather(coarse_sol, ("sub", "grp"), axis=0, tiled=True)
    pulled_flat = whole[flat_ids]
    pulled = pulled_flat.reshape(subs, slots_per, rcols) * live[:, :, None].astype(jnp.bfloat16)
    local = jnp.einsum("smn,srn->srm", local_inv, resid, preferred_element_type=jnp.float32)
    return local + jnp.einsum("smk,skr->srm", basis, pulled, preferred_element_type=jnp.float32)


def solution(mesh):
    placed = (
        P(("sub", "grp"), None, None),
        P(("sub", "grp"), None, None),
        P(("sub", "grp"), None, None),
        P(("sub", "grp"), None),
        P(("sub", "grp"), None),
        P(("sub", "grp")),
    )
    return jax.shard_map(
        per_device,
        mesh=mesh,
        in_specs=placed,
        out_specs=P(("sub", "grp"), None, None),
        check_vma=False,
    )
```

profile of v0, /device:TPU:1, one launch (start us, length us, event | category | flops | bytes accessed | tf_op | source)
XLA Modules:
  0.0 297.8 jit_solution(12218320992935361571)
XLA Ops:
  6.5 0.0 copy-start
  6.5 0.8 add_select_fusion
  7.4 0.2 convert_reduce_fusion
  7.6 4.4 %sort.17 = (s32[1024]{0:T(1024)}, s32[1024]{0:T(1024)S(1)}) sort(s32[1024]{0:T(1024)S(1)} %get-tuple-element.10, s32[1024]{0:T(1024)S(1)} %iota.25), dimensions={0}, to_apply=%region_0.1 | sort | flops 10240 | bytes 16384 | tf_op jit(solution)/shard_map/jit(argsort)/sort | solution.py:27
  12.0 4.5 %gather_fusion = s32[1024]{0:T(1024)S(1)} fusion(s32[1024]{0:T(1024)S(1)} %get-tuple-element.10, s32[1024]{0:T(1024)S(1)} %fusion.14), kind=kCustom, calls=%fused_computation | custom fusion | bytes 12288 | tf_op jit(solution)/shard_map/gather | solution.py:28
  16.5 0.1 copy.20
  16.6 0.2 reduce-window.9
  16.8 0.1 reduce
  16.9 6.6 %gather_fusion.1 = s32[1024]{0:T(1024)S(1)} fusion(s32[128]{0:T(128)S(1)} %sub.23, s32[1024]{0:T(1024)S(1)} %broadcast_clamp_fusion.1), kind=kCustom, calls=%fused_computation.1 | custom fusion | bytes 12288 | tf_op jit(solution)/shard_map/gather | solution.py:33
  23.5 0.0 copy-start.4
  23.5 0.0 copy-start.2
  23.5 4.5 %gather_fusion.2 = s32[1024]{0:T(1024)S(1)} fusion(s32[1024]{0:T(1024)S(1)} %get-tuple-element.9, s32[1024]{0:T(1024)S(1)} %fusion.14), kind=kCustom, calls=%fused_computation.2 | custom fusion | bytes 12288 | tf_op jit(solution)/shard_map/gather | solution.py:36
  28.1 4.3 %scatter_custom_fusion = s32[2048]{0:T(1024)S(1)} fusion(s32[1024]{0:T(1024)S(1)} %bitcast.62, s32[1024]{0:T(1024)S(1)} %gather_fusion.2, s32[]{:T(128)} %constant.34.clone.1), kind=kCustom, calls=%fused_computation.42 | custom fusion | bytes 8196 | tf_op jit(solution)/shard_map/scatter | solution.py:36
  32.4 0.7 all_to_all.9
  33.1 11.5 %all-to-all-start = ((s32[128,1,16]{2,1,0:T(1,128)}), s32[128,1,16]{2,1,0:T(1,128)S(1)}, u32[]{:S(2)}, u32[]{:S(2)}) async-start(s32[128,1,16]{2,1,0:T(1,128)} %bitcast.6), calls=%async_computation | async-start | bytes 131072 | tf_op jit(solution)/shard_map/all_to_all | solution.py:45
  44.6 0.0 copy-done.4
  44.6 0.1 fusion.21
  44.7 0.0 copy-done
  44.7 0.0 copy-done.2
  44.7 1.8 convolution_multiply_fusion
  46.5 13.2 %scatter_custom_fusion.1 = f32[2048,384]{1,0:T(8,128)} fusion(s32[1024]{0:T(1024)S(1)} %bitcast.63, f32[1024,384]{1,0:T(8,128)} %bitcast.55, s32[1024]{0:T(1024)S(1)} %fusion.14, f32[]{:T(128)} %constant.44.clone.1), kind=kCustom, calls=%fused_computation.14 | custom fusion | bytes 3146240 | tf_op jit(solution)/shard_map/scatter | solution.py:35
  59.7 0.0 all-to-all-done
  59.7 10.2 %all-to-all-start.1 = ((f32[128,16,384]{2,1,0:T(8,128)}), f32[128,16,384]{2,1,0:T(8,128)}, u32[]{:S(2)}, u32[]{:S(2)}) async-start(f32[128,16,384]{2,1,0:T(8,128)} %bitcast.53), calls=%async_computation.1 | async-start | bytes 6291456 | tf_op jit(solution)/shard_map/all_to_all | solution.py:38
  69.9 0.2 all-gather.2.cloned.1.call-start
  70.1 0.5 broadcast.152
  70.6 0.7 reduce.4
  71.3 0.1 eq.33
  71.4 40.3 %all-to-all-done.1 = f32[128,16,384]{2,1,0:T(8,128)} async-done(((f32[128,16,384]{2,1,0:T(8,128)}), f32[128,16,384]{2,1,0:T(8,128)}, u32[]{:S(2)}, u32[]{:S(2)}) %all-to-all-start.1) | async-done | bytes 3145760 | tf_op jit(solution)/shard_map/all_to_all | solution.py:38
  111.6 3.4 %fusion = (bf16[2048,384]{1,0:T(8,128)(2,1)S(1)}, bf16[2048,384]{1,0:T(8,128)(2,1)}) fusion(f32[128,16,384]{2,1,0:T(8,128)} %all-to-all-done.1), kind=kLoop, calls=%fused_computation.9 | loop fusion | flops 3145728 | bytes 6291456 | tf_op jit(solution)/shard_map/convert_element_type | solution.py:55
  115.0 0.0 copy-start.5
  115.0 1.1 fusion.1
  116.1 0.0 copy-done.5
  116.1 0.0 copy-start.3
  116.2 3.5 %fusion.8 = bf16[256,384]{0,1:T(8,128)(2,1)} fusion(bf16[256,256]{1,0:T(8,128)(2,1)S(1)} %copy-done.5, f32[256,384]{1,0:T(8,128)S(1)} %fusion.1, bf16[2048,384]{1,0:T(8,128)(2,1)} %get-tuple-element.8, s32[2048]{0:T(1024)S(1)} %eq.33), kind=kOutput, calls=%fused_computation.21 | convolution fusion | flops 453804032 | bytes 2301952 | tf_op jit(solution)/shard_map/dot_general | solution.py:62
  119.6 0.0 all-gather.2.cloned.1.call-update
  119.6 0.0 copy-done.3
  119.7 3.5 %fusion.22 = f32[8,384,256]{2,1,0:T(8,128)} fusion(bf16[8,384,256]{2,1,0:T(8,128)(2,1)S(1)} %copy-done, bf16[8,256,256]{2,1,0:T(8,128)(2,1)} %param.7), kind=kOutput, calls=%fused_computation.50 | convolution fusion | flops 402653184 | bytes 5767168 | tf_op jit(solution)/shard_map/smn,srn->srm/dot_general | solution.py:68
  123.2 115.4 %all-gather.2.cloned.1.call-done = bf16[32768,384]{0,1:T(8,128)(2,1)} async-done(((bf16[256,384]{0,1:T(8,128)(2,1)}), bf16[32768,384]{0,1:T(8,128)(2,1)}) %all-gather.2.cloned.1.call-update) | async-done | bytes 25165840 | tf_op jit(solution)/shard_map/all_gather | solution.py:65
  238.6 32.6 %copy.23 = bf16[32768,384]{1,0:T(8,128)(2,1)} copy(bf16[32768,384]{0,1:T(8,128)(2,1)} %all-gather.2.cloned.1.call-done) | data formatting | bytes 50331648 | tf_op jit(solution)/shard_map/all_gather | solution.py:65
  271.2 15.2 %gather_fusion.3 = bf16[1024,384]{1,0:T(8,128)(2,1)S(1)} fusion(bf16[32768,384]{1,0:T(8,128)(2,1)} %copy.23, s32[1024]{0:T(1024)S(1)} %broadcast_clamp_fusion), kind=kCustom, calls=%fused_computation.4 | custom fusion | bytes 1576960 | tf_op jit(solution)/shard_map/gather | solution.py:66
  286.4 0.4 copy.24
  286.7 0.0 copy-start.1
  286.7 4.3 %convolution_add_fusion = f32[8,384,256]{2,1,0:T(8,128)} fusion(f32[8,384,256]{2,1,0:T(8,128)} %fusion.22, bf16[8,256,128]{2,1,0:T(8,128)(2,1)S(1)} %copy-done.2, bf16[8,128,384]{1,2,0:T(8,128)(2,1)S(1)} %copy.24, bf16[8,128]{1,0:T(8,128)(2,1)S(1)} %get-tuple-element.11), kind=kOutput, calls=%fused_computation.13 | convolution fusion | flops 202506240 | bytes 7604224 | tf_op jit(solution)/shard_map/smk,skr->srm/dot_general | solution.py:69
  291.0 0.0 copy-done.1
  (8 shorter events, 0.1 us)
Async XLA Ops:
  6.5 38.2 %copy-start = (bf16[8,384,256]{2,1,0:T(8,128)(2,1)S(1)}, bf16[8,384,256]{2,1,0:T(8,128)(2,1)}, u32[]{:S(2)}) copy-start(bf16[8,384,256]{2,1,0:T(8,128)(2,1)} %param.6) | copy-start | bytes 4718596
  23.5 21.1 %copy-start.4 = (s32[8]{0:T(128)S(1)}, s32[8]{0:T(128)}, u32[]{:S(2)}) copy-start(s32[8]{0:T(128)} %param.11) | copy-start | bytes 100
  23.5 21.2 %copy-start.2 = (bf16[8,256,128]{2,1,0:T(8,128)(2,1)S(1)}, bf16[8,256,128]{2,1,0:T(8,128)(2,1)}, u32[]{:S(2)}) copy-start(bf16[8,256,128]{2,1,0:T(8,128)(2,1)} %param.8) | copy-start | bytes 1572868
  33.1 26.6 %all-to-all-start = ((s32[128,1,16]{2,1,0:T(1,128)}), s32[128,1,16]{2,1,0:T(1,128)S(1)}, u32[]{:S(2)}, u32[]{:S(2)}) async-start(s32[128,1,16]{2,1,0:T(1,128)} %bitcast.6), calls=%async_computation | async-start | bytes 131072 | tf_op jit(solution)/shard_map/all_to_all | solution.py:45
  59.7 51.9 %all-to-all-start.1 = ((f32[128,16,384]{2,1,0:T(8,128)}), f32[128,16,384]{2,1,0:T(8,128)}, u32[]{:S(2)}, u32[]{:S(2)}) async-start(f32[128,16,384]{2,1,0:T(8,128)} %bitcast.53), calls=%async_computation.1 | async-start | bytes 6291456 | tf_op jit(solution)/shard_map/all_to_all | solution.py:38
  69.9 168.7 %all-gather.2.cloned.1.call-start = ((), (), s32[]{:S(2)}) async-start(), calls=%async_computation.2 | async-start | bytes 25362432 | tf_op jit(solution)/shard_map/all_gather | solution.py:65
  115.0 1.1 copy-start.5
  116.1 3.5 %copy-start.3 = (s32[8,128]{1,0:T(8,128)S(1)}, s32[8,128]{1,0:T(8,128)}, u32[]{:S(2)}) copy-start(s32[8,128]{1,0:T(8,128)} %param.10) | copy-start | bytes 12292
  286.7 4.3 %copy-start.1 = (bf16[8,384,256]{2,1,0:T(8,128)(2,1)S(1)}, bf16[8,384,256]{2,1,0:T(8,128)(2,1)}, u32[]{:S(2)}) copy-start(bf16[8,384,256]{2,1,0:T(8,128)(2,1)} %param.6) | copy-start | bytes 4718596
Sparse Core Ops, SparseCore 0:
  119.8 118.7 all-gather.1
where the time goes:
time: 299 us; the launch traced here: 298 us
  waiting for transfers between devices  156 us (52%)
  local copies, waits for them, and re-layouts  82.7 us (28%)
  starting transfers between devices  21.9 us (7%)
  matrix products  14.1 us (5%)
  between operations  13.6 us (5%)
  other arithmetic  9.89 us (3%)
    all_gather x1, waiting for transfers between devices, per_device(): whole = lax.all_gather(coarse_sol, ('sub', 'grp'), axis=0, tiled=True)  115 us
    all_to_all x1, waiting for transfers between devices, per_device(): lax.all_to_all(send_vals.reshape(owners, cap, rcols), ('sub', 'grp'), spl...  40.3 us
    all_gather x1, local copies, waits for them, and re-layouts, per_device(): whole = lax.all_gather(coarse_sol, ('sub', 'grp'), axis=0, tiled=True)  32.6 us
    gather x1, local copies, waits for them, and re-layouts, per_device(): pulled_flat = whole[flat_ids]  15.2 us
    scatter x1, local copies, waits for them, and re-layouts, per_device(): jnp.zeros((owners * cap, rcols), jnp.float32).at[slot_index]  13.2 us
    all_to_all x1, starting transfers between devices, per_device(): lax.all_to_all(send_ids.reshape(owners, cap), ('sub', 'grp'), split_axis=...  11.5 us
    all_to_all x1, starting transfers between devices, per_device(): lax.all_to_all(send_vals.reshape(owners, cap, rcols), ('sub', 'grp'), spl...  10.2 us
    gather x1, local copies, waits for them, and re-layouts, per_device(): position = jnp.arange(slots, dtype=jnp.int32) - offsets[sorted_target]  6.57 us
  transfers between devices with their start and end apart: 3, of which 2 were waited for; matrix products, arithmetic and copies ran while one was open for 7% of the time, Pallas kernels for 0%

commit v1 on v0

v1 whole, which is shorter than its diff:
```python
import functools

import jax
import jax.numpy as jnp
from jax import lax
from jax.experimental import pallas as pl
from jax.experimental.pallas import tpu as pltpu
from jax.sharding import PartitionSpec as P

CAP = 16
LANES = 128
IDROWS = 8
F32 = jnp.float32
BF16 = jnp.bfloat16
AXES = ("sub", "grp")
NT = (((1,), (1,)), ((), ()))
TN = (((0,), (0,)), ((), ()))


def iota(shape, axis):
    return lax.broadcasted_iota(jnp.int32, shape, axis)


def dot(a, b, dims=(((1,), (0,)), ((), ()))):
    return lax.dot_general(a, b, dims, preferred_element_type=F32)


def pack_kernel(
    me_ref, counts_ref, map_ref, resid_hbm, basis_hbm, send_hbm, slot_ref,
    resid_v, basis_v, rest_v, send_v, in_sem, out_sem,
):
    subs, rcols, _ = resid_hbm.shape
    slots_per = basis_hbm.shape[2]
    owners = send_hbm.shape[0]
    blocks = rcols // LANES
    loads = []
    for s in range(subs):
        pair = (
            pltpu.make_async_copy(basis_hbm.at[s], basis_v.at[s], in_sem.at[0, s]),
            pltpu.make_async_copy(resid_hbm.at[s], resid_v.at[s], in_sem.at[1, s]),
        )
        for copy in pair:
            copy.start()
        loads.append(pair)

    lane = iota((1, slots_per), 1)
    row = iota((owners, slots_per), 0)
    before = jnp.where(
        iota((slots_per, 2 * slots_per), 0) < iota((slots_per, 2 * slots_per), 1), 1.0, 0.0
    ).astype(BF16)
    group = lax.rem(me_ref[0], LANES // CAP)
    id_place = jnp.where(row // CAP == group, lax.rem(row, CAP), -1)
    taken = jnp.zeros((owners, slots_per), F32)
    table = jnp.zeros((owners, LANES), F32)
    slot_rows = []
    for s in range(subs):
        ids = map_ref[s : s + 1, :]
        live = lane < counts_ref[s]
        target = jnp.where(live, ids // 256, -1)
        within = lax.rem(ids, 256) + 1
        hit = row == target
        onehot = jnp.where(hit, 1.0, 0.0).astype(BF16)
        sums = dot(onehot, before)
        rank = jnp.sum(jnp.where(hit, sums[:, :slots_per] + taken, 0.0), axis=0, keepdims=True)
        taken = taken + sums[:, slots_per:]
        rank = rank.astype(jnp.int32)
        named = jnp.where(id_place == rank, within, 0).astype(F32).astype(BF16)
        table = table + dot(onehot, named, NT)
        slot = jnp.where(live, target * CAP + rank, -1)
        slot_ref[s : s + 1, :] = slot
        slot_rows.append(slot)
    send_v[:, blocks * CAP :, :] = jnp.broadcast_to(
        table[:, None, :], (owners, IDROWS, LANES)
    ).astype(BF16)

    for s in range(subs):
        for copy in loads[s]:
            copy.wait()
        rest_v[:, s * slots_per : (s + 1) * slots_per] = dot(resid_v[s], basis_v[s]).astype(BF16)

    tile = LANES // CAP * 2
    slots = jnp.concatenate(slot_rows, axis=1)
    place = iota((tile * CAP, slots.shape[1]), 0)
    stores = []
    for t in range(owners // tile):
        pick = jnp.where(place == slots - t * tile * CAP, 1.0, 0.0).astype(BF16)
        part = dot(pick, rest_v[...], NT).astype(BF16).reshape(tile, CAP, rcols)
        for q in range(blocks):
            send_v[t * tile : (t + 1) * tile, q * CAP : (q + 1) * CAP, :] = part[
                :, :, q * LANES : (q + 1) * LANES
            ]
        copy = pltpu.make_async_copy(
            send_v.at[pl.ds(t * tile, tile)], send_hbm.at[pl.ds(t * tile, tile)], out_sem.at[t]
        )
        copy.start()
        stores.append(copy)
    for copy in stores:
        copy.wait()


def owner_kernel(recv_hbm, inv_ref, back_hbm, recv_v, back_v, match_v, in_sem, out_sem):
    owners = recv_hbm.shape[0]
    rcols = back_hbm.shape[2]
    blocks = rcols // LANES
    cblock = inv_ref.shape[0]
    tile = LANES // CAP * 2
    rows = tile * CAP
    tiles = owners // tile
    loads = []
    for t in range(tiles):
        copy = pltpu.make_async_copy(
            recv_hbm.at[pl.ds(t * tile, tile)], recv_v.at[pl.ds(t * tile, tile)], in_sem.at[t]
        )
        copy.start()
        loads.append(copy)
    dof = iota((cblock, LANES), 0) + 1
    total = jnp.zeros((cblock, rcols), F32)
    for t in range(tiles):
        loads[t].wait()
        halves = []
        for h in range(2):
            start = t * tile + h * (tile // 2)
            named = recv_v[start : start + tile // 2, blocks * CAP :, :].astype(F32)
            named = jnp.sum(named, axis=0)[0:1, :].astype(jnp.int32)
            halves.append(jnp.where(dof == named, 1.0, 0.0).astype(BF16))
        match = jnp.concatenate(halves, axis=1)
        match_v[:, t * rows : (t + 1) * rows] = match
        got = jnp.concatenate(
            [
                recv_v[t * tile : (t + 1) * tile, q * CAP : (q + 1) * CAP, :].reshape(rows, LANES)
                for q in range(blocks)
            ],
            axis=1,
        )
        total = total + dot(match, got)
    sol = dot(inv_ref[...], total.astype(BF16)).astype(BF16)
    stores = []
    for t in range(tiles):
        part = dot(match_v[:, t * rows : (t + 1) * rows], sol, TN).astype(BF16)
        back_v[t * tile : (t + 1) * tile] = part.reshape(tile, CAP, rcols)
        copy = pltpu.make_async_copy(
            back_v.at[pl.ds(t * tile, tile)], back_hbm.at[pl.ds(t * tile, tile)], out_sem.at[t]
        )
        copy.start()
        stores.append(copy)
    for copy in stores:
        copy.wait()


def finish_kernel(
    back_hbm, slot_ref, resid_hbm, inv_hbm, basis_hbm, out_hbm,
    back_v, resid_v, inv_v, basis_v, pulled_v, out_v, back_sem, in_sem, out_sem,
):
    subs, rcols, _ = resid_hbm.shape
    slots_per = basis_hbm.shape[2]
    owners = back_hbm.shape[0]
    whole = pltpu.make_async_copy(back_hbm, back_v, back_sem)
    whole.start()
    loads = []
    for s in range(subs):
        group = (
            pltpu.make_async_copy(resid_hbm.at[s], resid_v.at[s], in_sem.at[0, s]),
            pltpu.make_async_copy(inv_hbm.at[s], inv_v.at[s], in_sem.at[1, s]),
            pltpu.make_async_copy(basis_hbm.at[s], basis_v.at[s], in_sem.at[2, s]),
        )
        for copy in group:
            copy.start()
        loads.append(group)
    whole.wait()
    back = back_v[...].reshape(owners * CAP, rcols)
    place = iota((owners * CAP, 2 * slots_per), 0)
    for s in range(0, subs, 2):
        slots = jnp.concatenate([slot_ref[s : s + 1, :], slot_ref[s + 1 : s + 2, :]], axis=1)
        pick = jnp.where(place == slots, 1.0, 0.0).astype(BF16)
        pulled_v[:, s * slots_per : (s + 2) * slots_per] = dot(back, pick, TN).astype(BF16)
    stores = []
    for s in range(subs):
        for copy in loads[s]:
            copy.wait()
        out_v[s] = dot(resid_v[s], inv_v[s], NT) + dot(
            pulled_v[:, s * slots_per : (s + 1) * slots_per], basis_v[s], NT
        )
        copy = pltpu.make_async_copy(out_v.at[s], out_hbm.at[s], out_sem.at[s])
        copy.start()
        stores.append(copy)
    for copy in stores:
        copy.wait()


ANY = pl.BlockSpec(memory_space=pl.ANY)
INVMEM = pl.BlockSpec(memory_space=pltpu.VMEM)
INSMEM = pl.BlockSpec(memory_space=pltpu.SMEM)


def per_device(resid, local_inv, basis, coarse_inv, coarse_map, row_counts):
    subs, rcols, width = resid.shape
    slots_per = basis.shape[2]
    slots = subs * slots_per
    owners = lax.axis_size("sub") * lax.axis_size("grp")
    blocks = rcols // LANES
    tiles = owners // (2 * LANES // CAP)
    sem = pltpu.SemaphoreType.DMA
    params = pltpu.CompilerParams(vmem_limit_bytes=40 * 1024 * 1024)
    me = lax.axis_index(AXES).astype(jnp.int32).reshape(1)
    packed = (owners, blocks * CAP + IDROWS, LANES)
    send, slot = pl.pallas_call(
        pack_kernel,
        out_shape=(
            jax.ShapeDtypeStruct(packed, BF16),
            jax.ShapeDtypeStruct((subs, slots_per), jnp.int32),
        ),
        in_specs=[INSMEM, INSMEM, INVMEM, ANY, ANY],
        out_specs=(ANY, INVMEM),
        scratch_shapes=[
            pltpu.VMEM(resid.shape, BF16),
            pltpu.VMEM(basis.shape, BF16),
            pltpu.VMEM((rcols, slots), BF16),
            pltpu.VMEM(packed, BF16),
            sem((2, subs)),
            sem((tiles,)),
        ],
        compiler_params=params,
        name="pack",
    )(me, row_counts, coarse_map, resid, basis)
    recv = lax.all_to_all(send, AXES, split_axis=0, concat_axis=0, tiled=True)
    chunk = (owners, CAP, rcols)
    back = pl.pallas_call(
        owner_kernel,
        out_shape=jax.ShapeDtypeStruct(chunk, BF16),
        in_specs=[ANY, INVMEM],
        out_specs=ANY,
        scratch_shapes=[
            pltpu.VMEM(packed, BF16),
            pltpu.VMEM(chunk, BF16),
            pltpu.VMEM((coarse_inv.shape[0], owners * CAP), BF16),
            sem((tiles,)),
            sem((tiles,)),
        ],
        compiler_params=params,
        name="owner",
    )(recv, coarse_inv)
    back = lax.all_to_all(back, AXES, split_axis=0, concat_axis=0, tiled=True)
    return pl.pallas_call(
        finish_kernel,
        out_shape=jax.ShapeDtypeStruct((subs, rcols, width), F32),
        in_specs=[ANY, INVMEM, ANY, ANY, ANY],
        out_specs=ANY,
        scratch_shapes=[
            pltpu.VMEM(chunk, BF16),
            pltpu.VMEM(resid.shape, BF16),
            pltpu.VMEM(local_inv.shape, BF16),
            pltpu.VMEM(basis.shape, BF16),
            pltpu.VMEM((rcols, slots), BF16),
            pltpu.VMEM((subs, rcols, width), F32),
            sem,
            sem((3, subs)),
            sem((subs,)),
        ],
        compiler_params=params,
        name="finish",
    )(back, slot, resid, local_inv, basis)


def solution(mesh):
    placed = (
        P(("sub", "grp"), None, None),
        P(("sub", "grp"), None, None),
        P(("sub", "grp"), None, None),
        P(("sub", "grp"), None),
        P(("sub", "grp"), None),
        P(("sub", "grp")),
    )
    return jax.shard_map(
        per_device,
        mesh=mesh,
        in_specs=placed,
        out_specs=P(("sub", "grp"), None, None),
        check_vma=False,
    )
```

time: 299 us -> 103 us (0.34)
  waiting for transfers between devices: 156 us -> 0 us
  local copies, waits for them, and re-layouts: 82.7 us -> 3.81 us
  blocking collectives: 0 us -> 68.1 us
  Pallas kernels: 0 us -> 30.5 us
  starting transfers between devices: 21.9 us -> 0 us
  matrix products: 14.1 us -> 0 us
  between operations: 13.6 us -> 0.06 us
  other arithmetic: 9.89 us -> 0 us
    all_gather x1 -> x0, waiting for transfers between devices: 115 us -> none  [per_device(): whole = lax.all_gather(coarse_sol, ('sub', 'grp'), axis=0, tiled=True)]
    all_to_all x0 -> x2, blocking collectives: none -> 68.1 us  [the longest x1 39.3 us: per_device(): recv = lax.all_to_all(send, AXES, split_axis=0, concat_axis=0, tiled=True)]
    all_to_all x2 -> x0, waiting for transfers between devices: 40.3 us -> none  [the longest x1 40.3 us: per_device(): lax.all_to_all(send_vals.reshape(owners, cap, rcols), ('sub', 'grp'), spl...]
    all_gather x1 -> x0, local copies, waits for them, and re-layouts: 32.6 us -> none  [per_device(): whole = lax.all_gather(coarse_sol, ('sub', 'grp'), axis=0, tiled=True)]
    gather x4 -> x0, local copies, waits for them, and re-layouts: 30.8 us -> none  [the longest x1 15.2 us: per_device(): pulled_flat = whole[flat_ids]]
    pallas_call x0 -> x3, Pallas kernels: none -> 30.5 us  [the longest x1 12.1 us: per_device(): pl.pallas_call(pack_kernel, out_shape=(jax.ShapeDtypeStruct(packed, BF16)...]
    all_to_all x2 -> x0, starting transfers between devices: 21.7 us -> none  [the longest x1 11.5 us: per_device(): lax.all_to_all(send_ids.reshape(owners, cap), ('sub', 'grp'), split_axis=...]
    scatter x2 -> x0, local copies, waits for them, and re-layouts: 17.5 us -> none  [the longest x1 13.2 us: per_device(): jnp.zeros((owners * cap, rcols), jnp.float32).at[slot_index]]
  transfers between devices with their start and end apart: 3 -> 0, of which waited for: 2 -> 0; matrix products, arithmetic and copies ran while one was open for 7% -> 0% of each run, Pallas kernels for 0% -> 0%
where the time goes in v1:
time: 103 us; the launch traced here: 102 us
  blocking collectives  68.1 us (66%)
  Pallas kernels  30.5 us (30%)
  local copies, waits for them, and re-layouts  3.81 us (4%)
    all_to_all x1, blocking collectives, per_device(): recv = lax.all_to_all(send, AXES, split_axis=0, concat_axis=0, tiled=True)  39.3 us
    all_to_all x1, blocking collectives, per_device(): back = lax.all_to_all(back, AXES, split_axis=0, concat_axis=0, tiled=True)  28.8 us
    pallas_call x1, Pallas kernels, per_device(): pl.pallas_call(pack_kernel, out_shape=(jax.ShapeDtypeStruct(packed, BF16)...  12.1 us
    pallas_call x1, Pallas kernels, per_device(): pl.pallas_call(finish_kernel, out_shape=jax.ShapeDtypeStruct((subs, rcols...  9.93 us
    pallas_call x1, Pallas kernels, per_device(): pl.pallas_call(owner_kernel, out_shape=jax.ShapeDtypeStruct(chunk, BF16),...  8.41 us
    unnamed x16, local copies, waits for them, and re-layouts  3.81 us

profile of v1, /device:TPU:1, one launch (start us, length us, event | category | flops | bytes accessed | tf_op | source)
XLA Modules:
  0.0 102.5 jit_solution(13077761614661950969)
XLA Ops:
  0.0 0.0 copy-start
  0.0 1.4 %copy-done = bf16[8,384,256]{2,1,0:T(8,128)(2,1)S(1)} copy-done((bf16[8,384,256]{2,1,0:T(8,128)(2,1)S(1)}, bf16[8,384,256]{2,1,0:T(8,128)(2,1)}, u32[]{:S(2)}) %copy-start) | copy-done | bytes 1572888
  1.4 0.0 copy-start.2
  1.4 1.0 %copy-done.2 = bf16[8,256,128]{2,1,0:T(8,128)(2,1)S(1)} copy-done((bf16[8,256,128]{2,1,0:T(8,128)(2,1)S(1)}, bf16[8,256,128]{2,1,0:T(8,128)(2,1)}, u32[]{:S(2)}) %copy-start.2) | copy-done | bytes 524312
  2.5 0.0 copy-start.6
  2.5 0.7 copy-done.6
  3.1 0.0 copy-start.7
  3.1 0.7 copy-done.7
  3.8 12.1 %pack.1 = (bf16[128,56,128]{2,1,0:T(8,128)(2,1)S(1)}, s32[8,128]{1,0:T(8,128)S(1)}) custom-call(s32[1]{0:T(128)} %bitcast.me_ref, s32[8]{0:T(128)S(1)} %copy-done.7, s32[8,128]{1,0:T(8,128)S(1)} %copy-done.6, bf16[8,384,256]{2,1,0:T(8,128)(2,1)S(1)} %copy-done, bf16[8,256,128]{2,1,0:T(8,128)(2,1)S(1)} %copy-done.2), custom_call_target="tpu_custom_call" | custom-call | tf_op jit(solution)/shard_map/pack/pallas_call | solution.py:206
  15.9 0.0 copy-start.5
  15.9 39.3 %all_to_all.10.recv_hbm = bf16[128,56,128]{2,1,0:T(8,128)(2,1)S(1)} all-to-all(bf16[128,56,128]{2,1,0:T(8,128)(2,1)S(1)} %get-tuple-element.7), channel_id=1, replica_groups=mesh['sub'=32,'grp'=4] {'sub','grp'}, dimensions={0} | all-to-all | bytes 3670016 | tf_op jit(solution)/shard_map/all_to_all | solution.py:225
  55.3 0.0 copy-done.5
  55.3 8.4 %owner.1 = bf16[128,16,384]{2,1,0:T(8,128)(2,1)S(1)} custom-call(bf16[128,56,128]{2,1,0:T(8,128)(2,1)S(1)} %all_to_all.10.recv_hbm, bf16[256,256]{1,0:T(8,128)(2,1)S(1)} %copy-done.5), custom_call_target="tpu_custom_call" | custom-call | tf_op jit(solution)/shard_map/owner/pallas_call | solution.py:227
  63.7 0.0 copy-start.1
  63.7 0.0 copy-start.3
  63.7 0.0 copy-start.4
  63.7 28.8 %all_to_all.11.back_hbm = bf16[128,16,384]{2,1,0:T(8,128)(2,1)S(1)} all-to-all(bf16[128,16,384]{2,1,0:T(8,128)(2,1)S(1)} %owner.1), channel_id=1, replica_groups=mesh['sub'=32,'grp'=4] {'sub','grp'}, dimensions={0} | all-to-all | bytes 3145728 | tf_op jit(solution)/shard_map/all_to_all | solution.py:242
  92.5 0.0 copy-done.1
  92.5 0.0 copy-done.3
  92.5 0.0 copy-done.4
  92.5 9.9 %finish.1 = f32[8,384,256]{2,1,0:T(8,128)} custom-call(bf16[128,16,384]{2,1,0:T(8,128)(2,1)S(1)} %all_to_all.11.back_hbm, s32[8,128]{1,0:T(8,128)S(1)} %get-tuple-element.8.slot_ref, bf16[8,384,256]{2,1,0:T(8,128)(2,1)S(1)} %copy-done.1, bf16[8,256,256]{2,1,0:T(8,128)(2,1)S(1)} %copy-done.4, bf16[8,256,128]{2,1,0:T(8,128)(2,1)S(1)} %copy-done.3), custom_call_target="tpu_custom_call" | custom-call | tf_op jit(solution)/shard_map/finish/pallas_call | solution.py:243
Async XLA Ops:
  0.0 1.4 %copy-start = (bf16[8,384,256]{2,1,0:T(8,128)(2,1)S(1)}, bf16[8,384,256]{2,1,0:T(8,128)(2,1)}, u32[]{:S(2)}) copy-start(bf16[8,384,256]{2,1,0:T(8,128)(2,1)} %resid_hbm.3) | copy-start | bytes 4718596
  1.4 1.0 %copy-start.2 = (bf16[8,256,128]{2,1,0:T(8,128)(2,1)S(1)}, bf16[8,256,128]{2,1,0:T(8,128)(2,1)}, u32[]{:S(2)}) copy-start(bf16[8,256,128]{2,1,0:T(8,128)(2,1)} %basis_hbm.3) | copy-start | bytes 1572868
  2.5 0.7 copy-start.6
  3.1 0.7 copy-start.7
  15.9 39.3 %copy-start.5 = (bf16[256,256]{1,0:T(8,128)(2,1)S(1)}, bf16[256,256]{1,0:T(8,128)(2,1)}, u32[]{:S(2)}) copy-start(bf16[256,256]{1,0:T(8,128)(2,1)} %inv_ref.1) | copy-start | bytes 393220
  63.7 28.8 %copy-start.1 = (bf16[8,384,256]{2,1,0:T(8,128)(2,1)S(1)}, bf16[8,384,256]{2,1,0:T(8,128)(2,1)}, u32[]{:S(2)}) copy-start(bf16[8,384,256]{2,1,0:T(8,128)(2,1)} %resid_hbm.3) | copy-start | bytes 4718596
  63.7 28.8 %copy-start.3 = (bf16[8,256,128]{2,1,0:T(8,128)(2,1)S(1)}, bf16[8,256,128]{2,1,0:T(8,128)(2,1)}, u32[]{:S(2)}) copy-start(bf16[8,256,128]{2,1,0:T(8,128)(2,1)} %basis_hbm.3) | copy-start | bytes 1572868
  63.7 28.8 %copy-start.4 = (bf16[8,256,256]{2,1,0:T(8,128)(2,1)S(1)}, bf16[8,256,256]{2,1,0:T(8,128)(2,1)}, u32[]{:S(2)}) copy-start(bf16[8,256,256]{2,1,0:T(8,128)(2,1)} %inv_hbm.1) | copy-start | bytes 3145732

commit v2 on v0

v2 whole, which is shorter than its diff:
```python
import jax
import jax.numpy as jnp
from jax import lax
from jax.experimental import pallas as pl
from jax.experimental.pallas import tpu as pltpu
from jax.sharding import PartitionSpec as P

CAP = 16
LANES = 128
IDROWS = 8
F32 = jnp.float32
BF16 = jnp.bfloat16
AXES = ("sub", "grp")
NT = (((1,), (1,)), ((), ()))
TN = (((0,), (0,)), ((), ()))


def iota(shape, axis):
    return lax.broadcasted_iota(jnp.int32, shape, axis)


def dot(a, b, dims=(((1,), (0,)), ((), ()))):
    return lax.dot_general(a, b, dims, preferred_element_type=F32)


def pack_kernel(
    me_ref, counts_hbm, map_hbm, resid_hbm, basis_hbm, send_ref, slot_ref,
    counts_v, map_v, resid_v, basis_v, rest_v, small_sem, in_sem,
):
    subs, rcols, _ = resid_hbm.shape
    slots_per = basis_hbm.shape[2]
    owners = send_ref.shape[0]
    blocks = rcols // LANES
    small = (
        pltpu.make_async_copy(map_hbm, map_v, small_sem.at[0]),
        pltpu.make_async_copy(counts_hbm, counts_v, small_sem.at[1]),
    )
    for copy in small:
        copy.start()
    loads = []
    for s in range(subs):
        pair = (
            pltpu.make_async_copy(basis_hbm.at[s], basis_v.at[s], in_sem.at[0, s]),
            pltpu.make_async_copy(resid_hbm.at[s], resid_v.at[s], in_sem.at[1, s]),
        )
        for copy in pair:
            copy.start()
        loads.append(pair)
    for copy in small:
        copy.wait()

    lane = iota((1, slots_per), 1)
    row = iota((owners, slots_per), 0)
    before = jnp.where(
        iota((slots_per, 2 * slots_per), 0) < iota((slots_per, 2 * slots_per), 1), 1.0, 0.0
    ).astype(BF16)
    group = lax.rem(me_ref[0], LANES // CAP)
    id_row = iota((LANES, slots_per), 0)
    id_place = jnp.where(id_row // CAP == group, lax.rem(id_row, CAP), -1)
    targets = [
        jnp.where(lane < counts_v[s], map_v[s : s + 1, :] // 256, -1) for s in range(subs)
    ]
    hits = [row == target for target in targets]
    onehot = jnp.concatenate([jnp.where(hit, 1.0, 0.0).astype(BF16) for hit in hits], axis=0)
    sums = dot(onehot, before)
    taken = jnp.zeros((owners, slots_per), F32)
    slot_rows = []
    for s in range(subs):
        own = sums[s * owners : (s + 1) * owners]
        rank = jnp.sum(jnp.where(hits[s], own[:, :slots_per] + taken, 0.0), axis=0, keepdims=True)
        taken = taken + own[:, slots_per:]
        rank = rank.astype(jnp.int32)
        within = lax.rem(map_v[s : s + 1, :], 256) + 1
        slot = jnp.where(targets[s] < 0, -1, targets[s] * CAP + rank)
        rest_v[rcols:, s * slots_per : (s + 1) * slots_per] = (
            jnp.where(id_place == rank, within, 0).astype(F32).astype(BF16)
        )
        slot_ref[s : s + 1, :] = slot
        slot_rows.append(slot)

    for s in range(subs):
        for copy in loads[s]:
            copy.wait()
        rest_v[:rcols, s * slots_per : (s + 1) * slots_per] = dot(
            resid_v[s], basis_v[s]
        ).astype(BF16)

    tile = LANES // CAP * 2
    slots = jnp.concatenate(slot_rows, axis=1)
    place = iota((tile * CAP, slots.shape[1]), 0)
    for t in range(owners // tile):
        pick = jnp.where(place == slots - t * tile * CAP, 1.0, 0.0).astype(BF16)
        part = dot(pick, rest_v[...], NT)
        mine = slice(t * tile, (t + 1) * tile)
        for q in range(blocks):
            send_ref[mine, q * CAP : (q + 1) * CAP, :] = (
                part[:, q * LANES : (q + 1) * LANES].astype(BF16).reshape(tile, CAP, LANES)
            )
        named = part[:, rcols:].reshape(tile, CAP // IDROWS, IDROWS, LANES)
        send_ref[mine, blocks * CAP :, :] = jnp.sum(named, axis=1).astype(BF16)


def owner_kernel(recv_ref, inv_ref, back_ref, got_v, match_v):
    owners, _, rcols = back_ref.shape
    blocks = rcols // LANES
    cblock = inv_ref.shape[0]
    step = LANES // CAP
    dof = iota((cblock, LANES), 0) + 1
    for t in range(owners // step):
        mine = slice(t * step, (t + 1) * step)
        rows = slice(t * LANES, (t + 1) * LANES)
        named = jnp.sum(recv_ref[mine, blocks * CAP :, :].astype(F32), axis=0)
        named = jnp.sum(named, axis=0, keepdims=True).astype(jnp.int32)
        match_v[:, rows] = jnp.where(dof == named, 1.0, 0.0).astype(BF16)
        for q in range(blocks):
            got_v[rows, q * LANES : (q + 1) * LANES] = recv_ref[
                mine, q * CAP : (q + 1) * CAP, :
            ].reshape(LANES, LANES)
    total = dot(match_v[...], got_v[...])
    sol = dot(inv_ref[...], total.astype(BF16)).astype(BF16)
    tile = 4 * step
    for t in range(owners // tile):
        part = dot(match_v[:, t * tile * CAP : (t + 1) * tile * CAP], sol, TN).astype(BF16)
        back_ref[t * tile : (t + 1) * tile] = part.reshape(tile, CAP, rcols)


def local_kernel(resid_ref, inv_ref, out_ref):
    for s in range(resid_ref.shape[0]):
        out_ref[s] = dot(resid_ref[s], inv_ref[s], NT)


def finish_kernel(back_ref, slot_ref, local_ref, basis_ref, out_hbm, pulled_v, out_v, out_sem):
    subs, rcols, _ = local_ref.shape
    slots_per = basis_ref.shape[2]
    owners = back_ref.shape[0]
    back = back_ref[...].reshape(owners * CAP, rcols)
    place = iota((owners * CAP, subs * slots_per), 0)
    slots = jnp.concatenate([slot_ref[s : s + 1, :] for s in range(subs)], axis=1)
    pick = jnp.where(place == slots, 1.0, 0.0).astype(BF16)
    pulled_v[...] = dot(back, pick, TN).astype(BF16)
    stores = []
    for s in range(subs):
        out_v[s] = local_ref[s] + dot(
            pulled_v[:, s * slots_per : (s + 1) * slots_per], basis_ref[s], NT
        )
        copy = pltpu.make_async_copy(out_v.at[s], out_hbm.at[s], out_sem.at[s])
        copy.start()
        stores.append(copy)
    for copy in stores:
        copy.wait()


ANY = pl.BlockSpec(memory_space=pl.ANY)
HBM = pl.BlockSpec(memory_space=pltpu.HBM)
INVMEM = pl.BlockSpec(memory_space=pltpu.VMEM)
INSMEM = pl.BlockSpec(memory_space=pltpu.SMEM)


def params(mib):
    return pltpu.CompilerParams(vmem_limit_bytes=mib * 1024 * 1024)


def pack(me, counts, cmap, resid, basis, owners):
    subs, rcols, _ = resid.shape
    slots_per = basis.shape[2]
    shape = (owners, rcols // LANES * CAP + IDROWS, LANES)
    return pl.pallas_call(
        pack_kernel,
        out_shape=(
            jax.ShapeDtypeStruct(shape, BF16),
            jax.ShapeDtypeStruct((subs, slots_per), jnp.int32),
        ),
        in_specs=[INSMEM, HBM, HBM, HBM, HBM],
        out_specs=(INVMEM, INVMEM),
        scratch_shapes=[
            pltpu.SMEM(counts.shape, jnp.int32),
            pltpu.VMEM(cmap.shape, jnp.int32),
            pltpu.VMEM(resid.shape, BF16),
            pltpu.VMEM(basis.shape, BF16),
            pltpu.VMEM((rcols + LANES, subs * slots_per), BF16),
            pltpu.SemaphoreType.DMA((2,)),
            pltpu.SemaphoreType.DMA((2, subs)),
        ],
        compiler_params=params(24),
        name="pack",
    )(me, counts, cmap, resid, basis)


def owner(recv, inv, rcols):
    owners = recv.shape[0]
    return pl.pallas_call(
        owner_kernel,
        out_shape=jax.ShapeDtypeStruct((owners, CAP, rcols), BF16),
        in_specs=[INVMEM, INVMEM],
        out_specs=INVMEM,
        scratch_shapes=[
            pltpu.VMEM((owners * CAP, rcols), BF16),
            pltpu.VMEM((inv.shape[0], owners * CAP), BF16),
        ],
        compiler_params=params(24),
        name="owner",
    )(recv, inv)


def local_solve(resid, inv):
    subs, rcols, width = resid.shape
    return pl.pallas_call(
        local_kernel,
        out_shape=jax.ShapeDtypeStruct(resid.shape, F32),
        in_specs=[INVMEM, INVMEM],
        out_specs=INVMEM,
        compiler_params=params(24),
        cost_estimate=pl.CostEstimate(
            flops=2 * subs * rcols * width * width,
            bytes_accessed=2 * (resid.size + inv.size) + 4 * resid.size,
            transcendentals=0,
        ),
        name="local",
    )(resid, inv)


def finish(back, slot, local, basis):
    subs, rcols, _ = local.shape
    slots_per = basis.shape[2]
    return pl.pallas_call(
        finish_kernel,
        out_shape=jax.ShapeDtypeStruct(local.shape, F32),
        in_specs=[INVMEM, INVMEM, INVMEM, INVMEM],
        out_specs=ANY,
        scratch_shapes=[
            pltpu.VMEM((rcols, subs * slots_per), BF16),
            pltpu.VMEM(local.shape, F32),
            pltpu.SemaphoreType.DMA((subs,)),
        ],
        compiler_params=params(32),
        name="finish",
    )(back, slot, local, basis)


def per_device(resid, local_inv, basis, coarse_inv, coarse_map, row_counts):
    owners = lax.axis_size("sub") * lax.axis_size("grp")
    me = lax.axis_index(AXES).astype(jnp.int32).reshape(1)
    send, slot = pack(me, row_counts, coarse_map, resid, basis, owners)
    recv = lax.all_to_all(send, AXES, split_axis=0, concat_axis=0, tiled=True)
    local = local_solve(resid, local_inv)
    back = owner(recv, coarse_inv, resid.shape[1])
    back = lax.all_to_all(back, AXES, split_axis=0, concat_axis=0, tiled=True)
    return finish(back, slot, local, basis)


def solution(mesh):
    placed = (
        P(("sub", "grp"), None, None),
        P(("sub", "grp"), None, None),
        P(("sub", "grp"), None, None),
        P(("sub", "grp"), None),
        P(("sub", "grp"), None),
        P(("sub", "grp")),
    )
    return jax.shard_map(
        per_device,
        mesh=mesh,
        in_specs=placed,
        out_specs=P(("sub", "grp"), None, None),
        check_vma=False,
    )
```

time: 299 us -> 90 us (0.30)
  waiting for transfers between devices: 156 us -> 21.8 us
  local copies, waits for them, and re-layouts: 82.7 us -> 7.46 us
  blocking collectives: 0 us -> 39.3 us
  starting transfers between devices: 21.9 us -> 4.85 us
  Pallas kernels: 0 us -> 16.1 us
  matrix products: 14.1 us -> 0 us
  between operations: 13.6 us -> 0.05 us
  other arithmetic: 9.89 us -> 0 us
    all_gather x1 -> x0, waiting for transfers between devices: 115 us -> none  [per_device(): whole = lax.all_gather(coarse_sol, ('sub', 'grp'), axis=0, tiled=True)]
    all_to_all x0 -> x1, blocking collectives: none -> 39.3 us  [per_device(): recv = lax.all_to_all(send, AXES, split_axis=0, concat_axis=0, tiled=True)]
    all_gather x1 -> x0, local copies, waits for them, and re-layouts: 32.6 us -> none  [per_device(): whole = lax.all_gather(coarse_sol, ('sub', 'grp'), axis=0, tiled=True)]
    gather x4 -> x0, local copies, waits for them, and re-layouts: 30.8 us -> none  [the longest x1 15.2 us: per_device(): pulled_flat = whole[flat_ids]]
    all_to_all x2 -> x1, waiting for transfers between devices: 40.3 us -> 21.8 us  [per_device(): back = lax.all_to_all(back, AXES, split_axis=0, concat_axis=0, tiled=True)]
    scatter x2 -> x0, local copies, waits for them, and re-layouts: 17.5 us -> none  [the longest x1 13.2 us: per_device(): jnp.zeros((owners * cap, rcols), jnp.float32).at[slot_index]]
    all_to_all x2 -> x1, starting transfers between devices: 21.7 us -> 4.85 us  [per_device(): back = lax.all_to_all(back, AXES, split_axis=0, concat_axis=0, tiled=True)]
    pallas_call x0 -> x4, Pallas kernels: none -> 16.1 us  [the longest x1 7.48 us: pack(): pl.pallas_call(pack_kernel, out_shape=(jax.ShapeDtypeStruct(shape, BF16),...]
  transfers between devices with their start and end apart: 3 -> 1, of which waited for: 2 -> 1; matrix products, arithmetic and copies ran while one was open for 7% -> 0% of each run, Pallas kernels for 0% -> 1%
where the time goes in v2:
time: 90 us; the launch traced here: 89.6 us
  blocking collectives  39.3 us (44%)
  waiting for transfers between devices  21.8 us (24%)
  Pallas kernels  16.1 us (18%)
  local copies, waits for them, and re-layouts  7.46 us (8%)
  starting transfers between devices  4.85 us (5%)
    all_to_all x1, blocking collectives, per_device(): recv = lax.all_to_all(send, AXES, split_axis=0, concat_axis=0, tiled=True)  39.3 us
    all_to_all x1, waiting for transfers between devices, per_device(): back = lax.all_to_all(back, AXES, split_axis=0, concat_axis=0, tiled=True)  21.8 us
    pallas_call x1, Pallas kernels, pack(): pl.pallas_call(pack_kernel, out_shape=(jax.ShapeDtypeStruct(shape, BF16),...  7.48 us
    unnamed x16, local copies, waits for them, and re-layouts  7.46 us
    pallas_call x1, Pallas kernels, finish(): pl.pallas_call(finish_kernel, out_shape=jax.ShapeDtypeStruct(local.shape,...  5.13 us
    all_to_all x1, starting transfers between devices, per_device(): back = lax.all_to_all(back, AXES, split_axis=0, concat_axis=0, tiled=True)  4.85 us
    pallas_call x1, Pallas kernels, owner(): pl.pallas_call(owner_kernel, out_shape=jax.ShapeDtypeStruct((owners, CAP,...  2.88 us
  transfers between devices with their start and end apart: 1, of which 1 were waited for; matrix products, arithmetic and copies ran while one was open for 0% of the time, Pallas kernels for 1%

profile of v2, /device:TPU:1, one launch (start us, length us, event | category | flops | bytes accessed | tf_op | source)
XLA Modules:
  0.0 89.6 jit_solution(16454380797861942465)
XLA Ops:
  0.0 0.0 copy-start
  0.0 1.4 %copy-done = bf16[8,384,256]{2,1,0:T(8,128)(2,1)S(1)} copy-done((bf16[8,384,256]{2,1,0:T(8,128)(2,1)S(1)}, bf16[8,384,256]{2,1,0:T(8,128)(2,1)}, u32[]{:S(2)}) %copy-start) | copy-done | bytes 1572888
  1.4 0.0 copy-start.2
  1.4 1.0 %copy-done.2 = bf16[8,256,128]{2,1,0:T(8,128)(2,1)S(1)} copy-done((bf16[8,256,128]{2,1,0:T(8,128)(2,1)S(1)}, bf16[8,256,128]{2,1,0:T(8,128)(2,1)}, u32[]{:S(2)}) %copy-start.2) | copy-done | bytes 524312
  2.5 0.0 copy-start.6
  2.5 0.7 copy-done.6
  3.1 0.0 copy-start.7
  3.1 0.7 copy-done.7
  3.8 7.5 %pack.1 = (bf16[128,56,128]{2,1,0:T(8,128)(2,1)S(1)}, s32[8,128]{1,0:T(8,128)S(1)}) custom-call(s32[1]{0:T(128)} %bitcast.me_ref, s32[8]{0:T(128)S(1)} %copy-done.7, s32[8,128]{1,0:T(8,128)S(1)} %copy-done.6, bf16[8,384,256]{2,1,0:T(8,128)(2,1)S(1)} %copy-done, bf16[8,256,128]{2,1,0:T(8,128)(2,1)S(1)} %copy-done.2), custom_call_target="tpu_custom_call" | custom-call | tf_op jit(solution)/shard_map/pack/pallas_call | solution.py:167
  11.3 0.0 copy-start.5
  11.3 39.3 %all_to_all.10.recv_ref = bf16[128,56,128]{2,1,0:T(8,128)(2,1)S(1)} all-to-all(bf16[128,56,128]{2,1,0:T(8,128)(2,1)S(1)} %get-tuple-element.7), channel_id=1, replica_groups=mesh['sub'=32,'grp'=4] {'sub','grp'}, dimensions={0} | all-to-all | bytes 3670016 | tf_op jit(solution)/shard_map/all_to_all | solution.py:244
  50.6 0.0 copy-done.5
  50.6 2.9 %owner.1 = bf16[128,16,384]{2,1,0:T(8,128)(2,1)} custom-call(bf16[128,56,128]{2,1,0:T(8,128)(2,1)S(1)} %all_to_all.10.recv_ref, bf16[256,256]{1,0:T(8,128)(2,1)S(1)} %copy-done.5), custom_call_target="tpu_custom_call" | custom-call | tf_op jit(solution)/shard_map/owner/pallas_call | solution.py:191
  53.5 4.8 %all-to-all-start.1 = ((bf16[128,16,384]{2,1,0:T(8,128)(2,1)}), bf16[128,16,384]{2,1,0:T(8,128)(2,1)}, u32[]{:S(2)}, u32[]{:S(2)}) async-start(bf16[128,16,384]{2,1,0:T(8,128)(2,1)} %owner.1), calls=%async_computation.1 | async-start | bytes 3145728 | tf_op jit(solution)/shard_map/all_to_all | solution.py:247
  58.4 0.0 copy-start.1
  58.4 1.4 %copy-done.1 = bf16[8,384,256]{2,1,0:T(8,128)(2,1)S(1)} copy-done((bf16[8,384,256]{2,1,0:T(8,128)(2,1)S(1)}, bf16[8,384,256]{2,1,0:T(8,128)(2,1)}, u32[]{:S(2)}) %copy-start.1) | copy-done | bytes 1572888
  59.8 0.0 copy-start.4
  59.8 1.2 %copy-done.4 = bf16[8,256,256]{2,1,0:T(8,128)(2,1)S(1)} copy-done((bf16[8,256,256]{2,1,0:T(8,128)(2,1)S(1)}, bf16[8,256,256]{2,1,0:T(8,128)(2,1)}, u32[]{:S(2)}) %copy-start.4) | copy-done | bytes 1048600
  61.0 0.6 local.1.local_ref
  61.6 21.8 %all-to-all-done.1.back_ref = bf16[128,16,384]{2,1,0:T(8,128)(2,1)} async-done(((bf16[128,16,384]{2,1,0:T(8,128)(2,1)}), bf16[128,16,384]{2,1,0:T(8,128)(2,1)}, u32[]{:S(2)}, u32[]{:S(2)}) %all-to-all-start.1) | async-done | bytes 1572896 | tf_op jit(solution)/shard_map/all_to_all | solution.py:247
  83.4 0.0 copy-start.3
  83.4 1.0 %copy-done.3 = bf16[8,256,128]{2,1,0:T(8,128)(2,1)S(1)} copy-done((bf16[8,256,128]{2,1,0:T(8,128)(2,1)S(1)}, bf16[8,256,128]{2,1,0:T(8,128)(2,1)}, u32[]{:S(2)}) %copy-start.3) | copy-done | bytes 524312
  84.5 5.1 %finish.1 = f32[8,384,256]{2,1,0:T(8,128)} custom-call(bf16[128,16,384]{2,1,0:T(8,128)(2,1)} %all-to-all-done.1.back_ref, s32[8,128]{1,0:T(8,128)S(1)} %get-tuple-element.8.slot_ref, f32[8,384,256]{2,1,0:T(8,128)S(1)} %local.1.local_ref, bf16[8,256,128]{2,1,0:T(8,128)(2,1)S(1)} %copy-done.3), custom_call_target="tpu_custom_call" | custom-call | tf_op jit(solution)/shard_map/finish/pallas_call | solution.py:225
Async XLA Ops:
  0.0 1.4 %copy-start = (bf16[8,384,256]{2,1,0:T(8,128)(2,1)S(1)}, bf16[8,384,256]{2,1,0:T(8,128)(2,1)}, u32[]{:S(2)}) copy-start(bf16[8,384,256]{2,1,0:T(8,128)(2,1)} %resid_ref.1) | copy-start | bytes 4718596
  1.4 1.0 %copy-start.2 = (bf16[8,256,128]{2,1,0:T(8,128)(2,1)S(1)}, bf16[8,256,128]{2,1,0:T(8,128)(2,1)}, u32[]{:S(2)}) copy-start(bf16[8,256,128]{2,1,0:T(8,128)(2,1)} %basis_ref.1) | copy-start | bytes 1572868
  2.5 0.7 copy-start.6
  3.1 0.7 copy-start.7
  11.3 39.3 %copy-start.5 = (bf16[256,256]{1,0:T(8,128)(2,1)S(1)}, bf16[256,256]{1,0:T(8,128)(2,1)}, u32[]{:S(2)}) copy-start(bf16[256,256]{1,0:T(8,128)(2,1)} %inv_ref.2) | copy-start | bytes 393220
  53.5 29.9 %all-to-all-start.1 = ((bf16[128,16,384]{2,1,0:T(8,128)(2,1)}), bf16[128,16,384]{2,1,0:T(8,128)(2,1)}, u32[]{:S(2)}, u32[]{:S(2)}) async-start(bf16[128,16,384]{2,1,0:T(8,128)(2,1)} %owner.1), calls=%async_computation.1 | async-start | bytes 3145728 | tf_op jit(solution)/shard_map/all_to_all | solution.py:247
  58.4 1.4 %copy-start.1 = (bf16[8,384,256]{2,1,0:T(8,128)(2,1)S(1)}, bf16[8,384,256]{2,1,0:T(8,128)(2,1)}, u32[]{:S(2)}) copy-start(bf16[8,384,256]{2,1,0:T(8,128)(2,1)} %resid_ref.1) | copy-start | bytes 4718596
  59.8 1.2 %copy-start.4 = (bf16[8,256,256]{2,1,0:T(8,128)(2,1)S(1)}, bf16[8,256,256]{2,1,0:T(8,128)(2,1)}, u32[]{:S(2)}) copy-start(bf16[8,256,256]{2,1,0:T(8,128)(2,1)} %inv_ref.3) | copy-start | bytes 3145732
  83.4 1.0 %copy-start.3 = (bf16[8,256,128]{2,1,0:T(8,128)(2,1)S(1)}, bf16[8,256,128]{2,1,0:T(8,128)(2,1)}, u32[]{:S(2)}) copy-start(bf16[8,256,128]{2,1,0:T(8,128)(2,1)} %basis_ref.1) | copy-start | bytes 1572868

commit v3 on v2

v3 whole, which is shorter than its diff:
```python
import jax
import jax.numpy as jnp
from jax import lax
from jax.experimental import pallas as pl
from jax.experimental.pallas import tpu as pltpu
from jax.sharding import PartitionSpec as P

CAP = 16
LANES = 128
IDROWS = 8
PACK_TILE = 16
OWNER_WIDE = 16
FINISH_BATCH = 8
F32 = jnp.float32
BF16 = jnp.bfloat16
AXES = ("sub", "grp")
NT = (((1,), (1,)), ((), ()))
TN = (((0,), (0,)), ((), ()))


def iota(shape, axis):
    return lax.broadcasted_iota(jnp.int32, shape, axis)


def dot(a, b, dims=(((1,), (0,)), ((), ()))):
    return lax.dot_general(a, b, dims, preferred_element_type=F32)


def pack_kernel(
    me_ref, counts_hbm, map_hbm, resid_hbm, basis_hbm, send_ref, slot_ref,
    counts_v, map_v, resid_v, basis_v, rest_v, row_v, small_sem, in_sem,
):
    subs, rcols, _ = resid_hbm.shape
    slots_per = basis_hbm.shape[2]
    owners = send_ref.shape[0]
    blocks = rcols // LANES
    small = (
        pltpu.make_async_copy(map_hbm, map_v, small_sem.at[0]),
        pltpu.make_async_copy(counts_hbm, counts_v, small_sem.at[1]),
    )
    for copy in small:
        copy.start()

    def loads(s):
        return (
            pltpu.make_async_copy(basis_hbm.at[s], basis_v.at[s], in_sem.at[0, s]),
            pltpu.make_async_copy(resid_hbm.at[s], resid_v.at[s], in_sem.at[1, s]),
        )

    for s in range(subs):
        for copy in loads(s):
            copy.start()
    for copy in small:
        copy.wait()

    lane = iota((1, slots_per), 1)
    row = iota((owners, slots_per), 0)
    before = jnp.where(
        iota((slots_per, 2 * slots_per), 0) < iota((slots_per, 2 * slots_per), 1), 1.0, 0.0
    ).astype(BF16)
    group = lax.rem(me_ref[0], LANES // CAP)
    id_row = iota((LANES, slots_per), 0)
    id_place = jnp.where(id_row // CAP == group, lax.rem(id_row, CAP), -1)
    targets = [
        jnp.where(lane < counts_v[s], map_v[s : s + 1, :] // 256, -1) for s in range(subs)
    ]
    hits = [row == target for target in targets]
    onehot = jnp.concatenate([jnp.where(hit, 1.0, 0.0).astype(BF16) for hit in hits], axis=0)
    sums = dot(onehot, before)
    taken = jnp.zeros((owners, slots_per), F32)
    for s in range(subs):
        own = sums[s * owners : (s + 1) * owners]
        rank = jnp.sum(jnp.where(hits[s], own[:, :slots_per] + taken, 0.0), axis=0, keepdims=True)
        taken = taken + own[:, slots_per:]
        rank = rank.astype(jnp.int32)
        within = lax.rem(map_v[s : s + 1, :], 256) + 1
        slot = jnp.where(targets[s] < 0, -1, targets[s] * CAP + rank)
        rest_v[rcols:, s * slots_per : (s + 1) * slots_per] = (
            jnp.where(id_place == rank, within, 0).astype(F32).astype(BF16)
        )
        slot_ref[s : s + 1, :] = slot
        row_v[:, s * slots_per : (s + 1) * slots_per] = jnp.broadcast_to(slot, (8, slots_per))

    @pl.loop(0, subs)
    def _(s):
        for copy in loads(s):
            copy.wait()
        columns = pl.ds(pl.multiple_of(s * slots_per, slots_per), slots_per)
        rest_v[:rcols, columns] = dot(resid_v[s], basis_v[s]).astype(BF16)

    tile = LANES // CAP * PACK_TILE

    @pl.loop(0, owners // tile)
    def _(t):
        place = iota((tile * CAP, subs * slots_per), 0)
        pick = jnp.where(place == row_v[0:1, :] - t * (tile * CAP), 1.0, 0.0).astype(BF16)
        part = dot(pick, rest_v[...], NT)
        mine = pl.ds(t * tile, tile)
        for q in range(blocks):
            send_ref[mine, q * CAP : (q + 1) * CAP, :] = (
                part[:, q * LANES : (q + 1) * LANES].astype(BF16).reshape(tile, CAP, LANES)
            )
        named = part[:, rcols:].reshape(tile, CAP // IDROWS, IDROWS, LANES)
        send_ref[mine, blocks * CAP :, :] = jnp.sum(named, axis=1).astype(BF16)


def owner_kernel(recv_ref, inv_ref, back_ref, got_v, match_v, total_v):
    owners, _, rcols = back_ref.shape
    blocks = rcols // LANES
    cblock = inv_ref.shape[0]
    step = LANES // CAP
    wide = OWNER_WIDE
    total_v[...] = jnp.zeros_like(total_v)

    @pl.loop(0, owners // (wide * step))
    def _(t):
        dof = iota((cblock, LANES), 0) + 1
        for u in range(wide):
            mine = pl.ds((t * wide + u) * step, step)
            rows = slice(u * LANES, (u + 1) * LANES)
            named = jnp.sum(recv_ref[mine, blocks * CAP :, :].astype(F32), axis=0)
            named = jnp.sum(named, axis=0, keepdims=True).astype(jnp.int32)
            match_v[t, :, rows] = jnp.where(dof == named, 1.0, 0.0).astype(BF16)
            for q in range(blocks):
                got_v[rows, q * LANES : (q + 1) * LANES] = recv_ref[
                    mine, q * CAP : (q + 1) * CAP, :
                ].reshape(LANES, LANES)
        total_v[...] += dot(match_v[t], got_v[...])

    sol = dot(inv_ref[...], total_v[...].astype(BF16)).astype(BF16)

    @pl.loop(0, owners // (wide * step))
    def _(t):
        part = dot(match_v[t], sol, TN).astype(BF16)
        back_ref[pl.ds(t * wide * step, wide * step)] = part.reshape(wide * step, CAP, rcols)


def finish_kernel(
    back_ref, slot_ref, resid_ref, inv_ref, basis_ref, out_hbm, turned_v, row_v, out_v, out_sem
):
    subs, rcols, _ = resid_ref.shape
    slots_per = basis_ref.shape[2]
    rows = back_ref.shape[0] * CAP
    turned_v[...] = back_ref[...].reshape(rows, rcols).T
    batch = FINISH_BATCH
    for s in range(subs):
        row_v[s // batch, :, s % batch * slots_per : (s % batch + 1) * slots_per] = (
            jnp.broadcast_to(slot_ref[s : s + 1, :], (8, slots_per))
        )

    def store(s):
        return pltpu.make_async_copy(out_v.at[s], out_hbm.at[s], out_sem.at[s])

    @pl.loop(0, subs // batch)
    def _(t):
        place = iota((rows, batch * slots_per), 0)
        pick = jnp.where(place == row_v[t, 0:1, :], 1.0, 0.0).astype(BF16)
        pulled = dot(turned_v[...], pick).astype(BF16)
        for i in range(batch):
            s = t * batch + i
            out_v[s] = dot(resid_ref[s], inv_ref[s], NT) + dot(
                pulled[:, i * slots_per : (i + 1) * slots_per], basis_ref[s], NT
            )
            store(s).start()

    for s in range(subs):
        store(s).wait()


ANY = pl.BlockSpec(memory_space=pl.ANY)
HBM = pl.BlockSpec(memory_space=pltpu.HBM)
INVMEM = pl.BlockSpec(memory_space=pltpu.VMEM)
INSMEM = pl.BlockSpec(memory_space=pltpu.SMEM)


def params(mib):
    return pltpu.CompilerParams(vmem_limit_bytes=mib * 1024 * 1024)


def pack(me, counts, cmap, resid, basis, owners):
    subs, rcols, _ = resid.shape
    slots_per = basis.shape[2]
    shape = (owners, rcols // LANES * CAP + IDROWS, LANES)
    return pl.pallas_call(
        pack_kernel,
        out_shape=(
            jax.ShapeDtypeStruct(shape, BF16),
            jax.ShapeDtypeStruct((subs, slots_per), jnp.int32),
        ),
        in_specs=[INSMEM, HBM, HBM, HBM, HBM],
        out_specs=(INVMEM, INVMEM),
        scratch_shapes=[
            pltpu.SMEM(counts.shape, jnp.int32),
            pltpu.VMEM(cmap.shape, jnp.int32),
            pltpu.VMEM(resid.shape, BF16),
            pltpu.VMEM(basis.shape, BF16),
            pltpu.VMEM((rcols + LANES, subs * slots_per), BF16),
            pltpu.VMEM((8, subs * slots_per), jnp.int32),
            pltpu.SemaphoreType.DMA((2,)),
            pltpu.SemaphoreType.DMA((2, subs)),
        ],
        compiler_params=params(24),
        name="pack",
    )(me, *[pltpu.with_memory_space_constraint(x, pltpu.HBM) for x in (counts, cmap, resid, basis)])


def owner(recv, inv, rcols):
    owners = recv.shape[0]
    return pl.pallas_call(
        owner_kernel,
        out_shape=jax.ShapeDtypeStruct((owners, CAP, rcols), BF16),
        in_specs=[INVMEM, INVMEM],
        out_specs=INVMEM,
        scratch_shapes=[
            pltpu.VMEM((OWNER_WIDE * LANES, rcols), BF16),
            pltpu.VMEM(
                (owners * CAP // (OWNER_WIDE * LANES), inv.shape[0], OWNER_WIDE * LANES), BF16
            ),
            pltpu.VMEM((inv.shape[0], rcols), F32),
        ],
        compiler_params=params(24),
        name="owner",
    )(recv, inv)


def finish(back, slot, resid, inv, basis):
    subs, rcols, _ = resid.shape
    rows = back.shape[0] * CAP
    return pl.pallas_call(
        finish_kernel,
        out_shape=jax.ShapeDtypeStruct(resid.shape, F32),
        in_specs=[INVMEM] * 5,
        out_specs=ANY,
        scratch_shapes=[
            pltpu.VMEM((rcols, rows), BF16),
            pltpu.VMEM((subs // FINISH_BATCH, 8, FINISH_BATCH * basis.shape[2]), jnp.int32),
            pltpu.VMEM(resid.shape, F32),
            pltpu.SemaphoreType.DMA((subs,)),
        ],
        compiler_params=params(32),
        name="finish",
    )(back, slot, resid, inv, basis)


def per_device(resid, local_inv, basis, coarse_inv, coarse_map, row_counts):
    owners = lax.axis_size("sub") * lax.axis_size("grp")
    me = lax.axis_index(AXES).astype(jnp.int32).reshape(1)
    send, slot = pack(me, row_counts, coarse_map, resid, basis, owners)
    recv = lax.all_to_all(send, AXES, split_axis=0, concat_axis=0, tiled=True)
    back = owner(recv, coarse_inv, resid.shape[1])
    back = lax.all_to_all(back, AXES, split_axis=0, concat_axis=0, tiled=True)
    return finish(back, slot, resid, local_inv, basis)


def solution(mesh):
    placed = (
        P(("sub", "grp"), None, None),
        P(("sub", "grp"), None, None),
        P(("sub", "grp"), None, None),
        P(("sub", "grp"), None),
        P(("sub", "grp"), None),
        P(("sub", "grp")),
    )
    return jax.shard_map(
        per_device,
        mesh=mesh,
        in_specs=placed,
        out_specs=P(("sub", "grp"), None, None),
        check_vma=False,
    )
```

time: 90 us -> 79.8 us (0.89)
  blocking collectives: 39.3 us -> 68.1 us
  waiting for transfers between devices: 21.8 us -> 0 us
  local copies, waits for them, and re-layouts: 7.46 us -> 0.03 us
  starting transfers between devices: 4.85 us -> 0 us
  Pallas kernels: 16.1 us -> 11.5 us
    all_to_all x0 -> x1, blocking collectives: none -> 28.8 us  [per_device(): back = lax.all_to_all(back, AXES, split_axis=0, concat_axis=0, tiled=True)]
    all_to_all x1 -> x0, waiting for transfers between devices: 21.8 us -> none  [per_device(): back = lax.all_to_all(back, AXES, split_axis=0, concat_axis=0, tiled=True)]
    unnamed x16 -> x8, local copies, waits for them, and re-layouts: 7.46 us -> 0.03 us
    all_to_all x1 -> x0, starting transfers between devices: 4.85 us -> none  [per_device(): back = lax.all_to_all(back, AXES, split_axis=0, concat_axis=0, tiled=True)]
    pallas_call x2 -> x1, Pallas kernels: 5.74 us -> 3.76 us  [finish(): pl.pallas_call(finish_kernel, out_shape=jax.ShapeDtypeStruct(resid.shape,...]
    pallas_call x1, Pallas kernels: 7.48 us -> 5.97 us  [pack(): pl.pallas_call(pack_kernel, out_shape=(jax.ShapeDtypeStruct(shape, BF16),...]
    pallas_call x1, Pallas kernels: 2.88 us -> 1.75 us  [owner(): pl.pallas_call(owner_kernel, out_shape=jax.ShapeDtypeStruct((owners, CAP,...]
  transfers between devices with their start and end apart: 1 -> 0, of which waited for: 1 -> 0; matrix products, arithmetic and copies ran while one was open for 0% -> 0% of each run, Pallas kernels for 1% -> 0%
where the time goes in v3:
time: 79.8 us; the launch traced here: 79.7 us
  blocking collectives  68.1 us (85%)
  Pallas kernels  11.5 us (14%)
    all_to_all x1, blocking collectives, per_device(): recv = lax.all_to_all(send, AXES, split_axis=0, concat_axis=0, tiled=True)  39.3 us
    all_to_all x1, blocking collectives, per_device(): back = lax.all_to_all(back, AXES, split_axis=0, concat_axis=0, tiled=True)  28.8 us
    pallas_call x1, Pallas kernels, pack(): pl.pallas_call(pack_kernel, out_shape=(jax.ShapeDtypeStruct(shape, BF16),...  5.97 us
    pallas_call x1, Pallas kernels, finish(): pl.pallas_call(finish_kernel, out_shape=jax.ShapeDtypeStruct(resid.shape,...  3.76 us
    pallas_call x1, Pallas kernels, owner(): pl.pallas_call(owner_kernel, out_shape=jax.ShapeDtypeStruct((owners, CAP,...  1.75 us

profile of v3, /device:TPU:1, one launch (start us, length us, event | category | flops | bytes accessed | tf_op | source)
XLA Modules:
  0.0 79.7 jit_solution(12364572152624022195)
XLA Ops:
  0.0 6.0 %pack.1 = (bf16[128,56,128]{2,1,0:T(8,128)(2,1)S(1)}, s32[8,128]{1,0:T(8,128)S(1)}) custom-call(s32[1]{0:T(128)} %bitcast.me_ref, s32[8]{0:T(128)} %counts_hbm.1, s32[8,128]{1,0:T(8,128)} %map_hbm.1, bf16[8,384,256]{2,1,0:T(8,128)(2,1)} %resid_ref.1, bf16[8,256,128]{2,1,0:T(8,128)(2,1)} %basis_ref.1), custom_call_target="tpu_custom_call" | custom-call | tf_op jit(solution)/shard_map/pack/pallas_call | solution.py:184
  6.0 0.0 copy-start.3
  6.0 39.3 %all_to_all.10.recv_ref = bf16[128,56,128]{2,1,0:T(8,128)(2,1)S(1)} all-to-all(bf16[128,56,128]{2,1,0:T(8,128)(2,1)S(1)} %get-tuple-element.7), channel_id=1, replica_groups=mesh['sub'=32,'grp'=4] {'sub','grp'}, dimensions={0} | all-to-all | bytes 3670016 | tf_op jit(solution)/shard_map/all_to_all | solution.py:249
  45.3 0.0 copy-done.3
  45.3 1.7 %owner.1 = bf16[128,16,384]{2,1,0:T(8,128)(2,1)S(1)} custom-call(bf16[128,56,128]{2,1,0:T(8,128)(2,1)S(1)} %all_to_all.10.recv_ref, bf16[256,256]{1,0:T(8,128)(2,1)S(1)} %copy-done.3), custom_call_target="tpu_custom_call" | custom-call | tf_op jit(solution)/shard_map/owner/pallas_call | solution.py:209
  47.1 0.0 copy-start
  47.1 0.0 copy-start.1
  47.1 0.0 copy-start.2
  47.1 28.8 %all_to_all.11.back_ref = bf16[128,16,384]{2,1,0:T(8,128)(2,1)S(1)} all-to-all(bf16[128,16,384]{2,1,0:T(8,128)(2,1)S(1)} %owner.1), channel_id=1, replica_groups=mesh['sub'=32,'grp'=4] {'sub','grp'}, dimensions={0} | all-to-all | bytes 3145728 | tf_op jit(solution)/shard_map/all_to_all | solution.py:251
  75.9 0.0 copy-done
  75.9 0.0 copy-done.1
  75.9 0.0 copy-done.2
  75.9 3.8 %finish.1 = f32[8,384,256]{2,1,0:T(8,128)} custom-call(bf16[128,16,384]{2,1,0:T(8,128)(2,1)S(1)} %all_to_all.11.back_ref, s32[8,128]{1,0:T(8,128)S(1)} %get-tuple-element.8.slot_ref, bf16[8,384,256]{2,1,0:T(8,128)(2,1)S(1)} %copy-done, bf16[8,256,256]{2,1,0:T(8,128)(2,1)S(1)} %copy-done.2, bf16[8,256,128]{2,1,0:T(8,128)(2,1)S(1)} %copy-done.1), custom_call_target="tpu_custom_call" | custom-call | tf_op jit(solution)/shard_map/finish/pallas_call | solution.py:229
Async XLA Ops:
  6.0 39.3 %copy-start.3 = (bf16[256,256]{1,0:T(8,128)(2,1)S(1)}, bf16[256,256]{1,0:T(8,128)(2,1)}, u32[]{:S(2)}) copy-start(bf16[256,256]{1,0:T(8,128)(2,1)} %inv_ref.2) | copy-start | bytes 393220
  47.1 28.8 %copy-start = (bf16[8,384,256]{2,1,0:T(8,128)(2,1)S(1)}, bf16[8,384,256]{2,1,0:T(8,128)(2,1)}, u32[]{:S(2)}) copy-start(bf16[8,384,256]{2,1,0:T(8,128)(2,1)} %resid_ref.1) | copy-start | bytes 4718596
  47.1 28.8 %copy-start.1 = (bf16[8,256,128]{2,1,0:T(8,128)(2,1)S(1)}, bf16[8,256,128]{2,1,0:T(8,128)(2,1)}, u32[]{:S(2)}) copy-start(bf16[8,256,128]{2,1,0:T(8,128)(2,1)} %basis_ref.1) | copy-start | bytes 1572868
  47.1 28.8 %copy-start.2 = (bf16[8,256,256]{2,1,0:T(8,128)(2,1)S(1)}, bf16[8,256,256]{2,1,0:T(8,128)(2,1)}, u32[]{:S(2)}) copy-start(bf16[8,256,256]{2,1,0:T(8,128)(2,1)} %inv_ref.3) | copy-start | bytes 3145732

commit v4 on v3

--- a/solution.py
+++ b/solution.py
@@ -8,7 +8,6 @@
 CAP = 16
 LANES = 128
 IDROWS = 8
-PACK_TILE = 16
 OWNER_WIDE = 16
 FINISH_BATCH = 8
 F32 = jnp.float32
@@ -28,28 +27,23 @@
 
 def pack_kernel(
     me_ref, counts_hbm, map_hbm, resid_hbm, basis_hbm, send_ref, slot_ref,
-    counts_v, map_v, resid_v, basis_v, rest_v, row_v, small_sem, in_sem,
+    counts_v, map_v, resid_v, basis_v, rest_v, comp_v, first_v, first_s, small_sem, in_sem, first_sem,
 ):
     subs, rcols, _ = resid_hbm.shape
     slots_per = basis_hbm.shape[2]
+    slots = subs * slots_per
     owners = send_ref.shape[0]
     blocks = rcols // LANES
     small = (
         pltpu.make_async_copy(map_hbm, map_v, small_sem.at[0]),
         pltpu.make_async_copy(counts_hbm, counts_v, small_sem.at[1]),
     )
-    for copy in small:
+    large = (
+        pltpu.make_async_copy(basis_hbm, basis_v, in_sem.at[0]),
+        pltpu.make_async_copy(resid_hbm, resid_v, in_sem.at[1]),
+    )
+    for copy in small + large:
         copy.start()
-
-    def loads(s):
-        return (
-            pltpu.make_async_copy(basis_hbm.at[s], basis_v.at[s], in_sem.at[0, s]),
-            pltpu.make_async_copy(resid_hbm.at[s], resid_v.at[s], in_sem.at[1, s]),
-        )
-
-    for s in range(subs):
-        for copy in loads(s):
-            copy.start()
     for copy in small:
         copy.wait()
 
@@ -62,46 +56,54 @@
     id_row = iota((LANES, slots_per), 0)
     id_place = jnp.where(id_row // CAP == group, lax.rem(id_row, CAP), -1)
     targets = [
-        jnp.where(lane < counts_v[s], map_v[s : s + 1, :] // 256, -1) for s in range(subs)
+        jnp.where(lane < counts_v[s], map_v[s : s + 1, :] // 256, owners) for s in range(subs)
     ]
     hits = [row == target for target in targets]
-    onehot = jnp.concatenate([jnp.where(hit, 1.0, 0.0).astype(BF16) for hit in hits], axis=0)
-    sums = dot(onehot, before)
+    onehots = [jnp.where(hit, 1.0, 0.0).astype(BF16) for hit in hits]
+    lower = jnp.concatenate(
+        [jnp.where(row > target, 1.0, 0.0).astype(BF16) for target in targets], axis=1
+    )
+    first = dot(lower, jnp.ones((slots, slots_per), BF16))
+    first_v[...] = dot(jnp.ones((8, slots), BF16), lower, NT).astype(jnp.int32)
+    place = pltpu.make_async_copy(first_v, first_s, first_sem)
+    place.start()
+    sums = dot(jnp.concatenate(onehots, axis=0), before)
     taken = jnp.zeros((owners, slots_per), F32)
+    named, packed_rows = [], []
     for s in range(subs):
         own = sums[s * owners : (s + 1) * owners]
         rank = jnp.sum(jnp.where(hits[s], own[:, :slots_per] + taken, 0.0), axis=0, keepdims=True)
+        start = jnp.sum(jnp.where(hits[s], first, 0.0), axis=0, keepdims=True)
         taken = taken + own[:, slots_per:]
         rank = rank.astype(jnp.int32)
+        dead = targets[s] == owners
         within = lax.rem(map_v[s : s + 1, :], 256) + 1
-        slot = jnp.where(targets[s] < 0, -1, targets[s] * CAP + rank)
-        rest_v[rcols:, s * slots_per : (s + 1) * slots_per] = (
-            jnp.where(id_place == rank, within, 0).astype(F32).astype(BF16)
-        )
-        slot_ref[s : s + 1, :] = slot
-        row_v[:, s * slots_per : (s + 1) * slots_per] = jnp.broadcast_to(slot, (8, slots_per))
-
-    @pl.loop(0, subs)
-    def _(s):
-        for copy in loads(s):
-            copy.wait()
-        columns = pl.ds(pl.multiple_of(s * slots_per, slots_per), slots_per)
-        rest_v[:rcols, columns] = dot(resid_v[s], basis_v[s]).astype(BF16)
-
-    tile = LANES // CAP * PACK_TILE
-
-    @pl.loop(0, owners // tile)
-    def _(t):
-        place = iota((tile * CAP, subs * slots_per), 0)
-        pick = jnp.where(place == row_v[0:1, :] - t * (tile * CAP), 1.0, 0.0).astype(BF16)
-        part = dot(pick, rest_v[...], NT)
-        mine = pl.ds(t * tile, tile)
+        named.append(jnp.where(id_place == rank, within, 0).astype(F32).astype(BF16))
+        slot_ref[s : s + 1, :] = jnp.where(dead, -1, targets[s] * CAP + rank)
+        packed_rows.append(jnp.where(dead, -1, start.astype(jnp.int32) + rank))
+    table = dot(jnp.concatenate(onehots, axis=1), jnp.concatenate(named, axis=1), NT)
+    send_ref[:, blocks * CAP :, :] = jnp.broadcast_to(
+        table[:, None, :], (owners, IDROWS, LANES)
+    ).astype(BF16)
+
+    for copy in large:
+        copy.wait()
+    for s in range(subs):
+        rest_v[:, s * slots_per : (s + 1) * slots_per] = dot(resid_v[s], basis_v[s]).astype(BF16)
+
+    pick = jnp.where(
+        iota((slots, slots), 0) == jnp.concatenate(packed_rows, axis=1), 1.0, 0.0
+    ).astype(BF16)
+    packed = dot(pick, rest_v[...], NT)
+    for q in range(blocks):
+        comp_v[q, :slots, :] = packed[:, q * LANES : (q + 1) * LANES]
+        comp_v[q, slots:, :] = jnp.zeros((CAP, LANES), F32)
+    place.wait()
+
+    for o in range(owners):
+        rows = pl.ds(first_s[0, o], CAP)
         for q in range(blocks):
-            send_ref[mine, q * CAP : (q + 1) * CAP, :] = (
-                part[:, q * LANES : (q + 1) * LANES].astype(BF16).reshape(tile, CAP, LANES)
-            )
-        named = part[:, rcols:].reshape(tile, CAP // IDROWS, IDROWS, LANES)
-        send_ref[mine, blocks * CAP :, :] = jnp.sum(named, axis=1).astype(BF16)
+            send_ref[o, q * CAP : (q + 1) * CAP, :] = comp_v[q, rows, :].astype(BF16)
 
 
 def owner_kernel(recv_ref, inv_ref, back_ref, got_v, match_v, total_v):
@@ -119,7 +121,7 @@
             mine = pl.ds((t * wide + u) * step, step)
             rows = slice(u * LANES, (u + 1) * LANES)
             named = jnp.sum(recv_ref[mine, blocks * CAP :, :].astype(F32), axis=0)
-            named = jnp.sum(named, axis=0, keepdims=True).astype(jnp.int32)
+            named = named[0:1, :].astype(jnp.int32)
             match_v[t, :, rows] = jnp.where(dof == named, 1.0, 0.0).astype(BF16)
             for q in range(blocks):
                 got_v[rows, q * LANES : (q + 1) * LANES] = recv_ref[
@@ -194,10 +196,13 @@
             pltpu.VMEM(cmap.shape, jnp.int32),
             pltpu.VMEM(resid.shape, BF16),
             pltpu.VMEM(basis.shape, BF16),
-            pltpu.VMEM((rcols + LANES, subs * slots_per), BF16),
-            pltpu.VMEM((8, subs * slots_per), jnp.int32),
+            pltpu.VMEM((rcols, subs * slots_per), BF16),
+            pltpu.VMEM((rcols // LANES, subs * slots_per + CAP, LANES), F32),
+            pltpu.VMEM((8, owners), jnp.int32),
+            pltpu.SMEM((8, owners), jnp.int32),
             pltpu.SemaphoreType.DMA((2,)),
-            pltpu.SemaphoreType.DMA((2, subs)),
+            pltpu.SemaphoreType.DMA((2,)),
+            pltpu.SemaphoreType.DMA,
         ],
         compiler_params=params(24),
         name="pack",

time: 79.8 us -> 77.4 us (0.970)
  Pallas kernels: 11.5 us -> 8.99 us
    pallas_call x1, Pallas kernels: 5.97 us -> 3.52 us  [pack(): pl.pallas_call(pack_kernel, out_shape=(jax.ShapeDtypeStruct(shape, BF16),...]
where the time goes in v4:
time: 77.4 us; the launch traced here: 77.2 us
  blocking collectives  68.1 us (88%)
  Pallas kernels  8.99 us (12%)
    all_to_all x1, blocking collectives, per_device(): recv = lax.all_to_all(send, AXES, split_axis=0, concat_axis=0, tiled=True)  39.3 us
    all_to_all x1, blocking collectives, per_device(): back = lax.all_to_all(back, AXES, split_axis=0, concat_axis=0, tiled=True)  28.8 us
    pallas_call x1, Pallas kernels, finish(): pl.pallas_call(finish_kernel, out_shape=jax.ShapeDtypeStruct(resid.shape,...  3.76 us
    pallas_call x1, Pallas kernels, pack(): pl.pallas_call(pack_kernel, out_shape=(jax.ShapeDtypeStruct(shape, BF16),...  3.52 us
    pallas_call x1, Pallas kernels, owner(): pl.pallas_call(owner_kernel, out_shape=jax.ShapeDtypeStruct((owners, CAP,...  1.72 us

profile of v4, /device:TPU:1, one launch (start us, length us, event | category | flops | bytes accessed | tf_op | source)
XLA Modules:
  0.0 77.2 jit_solution(16254527974849882060)
XLA Ops:
  0.0 3.5 %pack.1 = (bf16[128,56,128]{2,1,0:T(8,128)(2,1)S(1)}, s32[8,128]{1,0:T(8,128)S(1)}) custom-call(s32[1]{0:T(128)} %bitcast.me_ref, s32[8]{0:T(128)} %counts_hbm.1, s32[8,128]{1,0:T(8,128)} %map_hbm.1, bf16[8,384,256]{2,1,0:T(8,128)(2,1)} %resid_ref.1, bf16[8,256,128]{2,1,0:T(8,128)(2,1)} %basis_ref.1), custom_call_target="tpu_custom_call" | custom-call | tf_op jit(solution)/shard_map/pack/pallas_call | solution.py:186
  3.5 0.0 copy-start.3
  3.5 39.3 %all_to_all.10.recv_ref = bf16[128,56,128]{2,1,0:T(8,128)(2,1)S(1)} all-to-all(bf16[128,56,128]{2,1,0:T(8,128)(2,1)S(1)} %get-tuple-element.7), channel_id=1, replica_groups=mesh['sub'=32,'grp'=4] {'sub','grp'}, dimensions={0} | all-to-all | bytes 3670016 | tf_op jit(solution)/shard_map/all_to_all | solution.py:254
  42.9 0.0 copy-done.3
  42.9 1.7 %owner.1 = bf16[128,16,384]{2,1,0:T(8,128)(2,1)S(1)} custom-call(bf16[128,56,128]{2,1,0:T(8,128)(2,1)S(1)} %all_to_all.10.recv_ref, bf16[256,256]{1,0:T(8,128)(2,1)S(1)} %copy-done.3), custom_call_target="tpu_custom_call" | custom-call | tf_op jit(solution)/shard_map/owner/pallas_call | solution.py:214
  44.6 0.0 copy-start
  44.6 0.0 copy-start.1
  44.6 0.0 copy-start.2
  44.6 28.8 %all_to_all.11.back_ref = bf16[128,16,384]{2,1,0:T(8,128)(2,1)S(1)} all-to-all(bf16[128,16,384]{2,1,0:T(8,128)(2,1)S(1)} %owner.1), channel_id=1, replica_groups=mesh['sub'=32,'grp'=4] {'sub','grp'}, dimensions={0} | all-to-all | bytes 3145728 | tf_op jit(solution)/shard_map/all_to_all | solution.py:256
  73.4 0.0 copy-done
  73.4 0.0 copy-done.1
  73.4 0.0 copy-done.2
  73.4 3.8 %finish.1 = f32[8,384,256]{2,1,0:T(8,128)} custom-call(bf16[128,16,384]{2,1,0:T(8,128)(2,1)S(1)} %all_to_all.11.back_ref, s32[8,128]{1,0:T(8,128)S(1)} %get-tuple-element.8.slot_ref, bf16[8,384,256]{2,1,0:T(8,128)(2,1)S(1)} %copy-done, bf16[8,256,256]{2,1,0:T(8,128)(2,1)S(1)} %copy-done.2, bf16[8,256,128]{2,1,0:T(8,128)(2,1)S(1)} %copy-done.1), custom_call_target="tpu_custom_call" | custom-call | tf_op jit(solution)/shard_map/finish/pallas_call | solution.py:234
Async XLA Ops:
  3.5 39.3 %copy-start.3 = (bf16[256,256]{1,0:T(8,128)(2,1)S(1)}, bf16[256,256]{1,0:T(8,128)(2,1)}, u32[]{:S(2)}) copy-start(bf16[256,256]{1,0:T(8,128)(2,1)} %inv_ref.2) | copy-start | bytes 393220
  44.6 28.8 %copy-start = (bf16[8,384,256]{2,1,0:T(8,128)(2,1)S(1)}, bf16[8,384,256]{2,1,0:T(8,128)(2,1)}, u32[]{:S(2)}) copy-start(bf16[8,384,256]{2,1,0:T(8,128)(2,1)} %resid_ref.1) | copy-start | bytes 4718596
  44.6 28.8 %copy-start.1 = (bf16[8,256,128]{2,1,0:T(8,128)(2,1)S(1)}, bf16[8,256,128]{2,1,0:T(8,128)(2,1)}, u32[]{:S(2)}) copy-start(bf16[8,256,128]{2,1,0:T(8,128)(2,1)} %basis_ref.1) | copy-start | bytes 1572868
  44.6 28.8 %copy-start.2 = (bf16[8,256,256]{2,1,0:T(8,128)(2,1)S(1)}, bf16[8,256,256]{2,1,0:T(8,128)(2,1)}, u32[]{:S(2)}) copy-start(bf16[8,256,256]{2,1,0:T(8,128)(2,1)} %inv_ref.3) | copy-start | bytes 3145732

commit v5 on v4

v5 whole, which is shorter than its diff:
```python
import jax
import jax.numpy as jnp
from jax import lax
from jax.experimental import pallas as pl
from jax.experimental.pallas import tpu as pltpu
from jax.sharding import PartitionSpec as P

CAP = 16
LANES = 128
IDROWS = 4
FINISH_BATCH = 4
F32 = jnp.float32
BF16 = jnp.bfloat16
AXES = ("sub", "grp")
NT = (((1,), (1,)), ((), ()))
TN = (((0,), (0,)), ((), ()))


def iota(shape, axis):
    return lax.broadcasted_iota(jnp.int32, shape, axis)


def dot(a, b, dims=(((1,), (0,)), ((), ()))):
    return lax.dot_general(a, b, dims, preferred_element_type=F32)


def pack_kernel(
    me_ref, counts_hbm, map_hbm, resid_hbm, basis_hbm, send_ref, slot_ref, first_ref,
    counts_v, map_v, resid_v, basis_v, rest_v, comp_v, table_v, first_s, small_sem, in_sem, first_sem,
):
    subs, rcols, _ = resid_hbm.shape
    slots_per = basis_hbm.shape[2]
    slots = subs * slots_per
    owners = send_ref.shape[0]
    blocks = rcols // LANES
    small = (
        pltpu.make_async_copy(map_hbm, map_v, small_sem.at[0]),
        pltpu.make_async_copy(counts_hbm, counts_v, small_sem.at[1]),
    )
    large = (
        pltpu.make_async_copy(basis_hbm, basis_v, in_sem.at[0]),
        pltpu.make_async_copy(resid_hbm, resid_v, in_sem.at[1]),
    )
    for copy in small + large:
        copy.start()
    for copy in small:
        copy.wait()

    lane = iota((1, slots_per), 1)
    row = iota((owners, slots_per), 0)
    before = jnp.where(
        iota((slots_per, 2 * slots_per), 0) < iota((slots_per, 2 * slots_per), 1), 1.0, 0.0
    ).astype(BF16)
    group = lax.rem(me_ref[0], LANES // CAP)
    id_row = iota((LANES, slots_per), 0)
    id_place = jnp.where(id_row // CAP == group, lax.rem(id_row, CAP), -1)
    targets = [
        jnp.where(lane < counts_v[s], map_v[s : s + 1, :] // 256, owners) for s in range(subs)
    ]
    hits = [row == target for target in targets]
    onehots = [jnp.where(hit, 1.0, 0.0).astype(BF16) for hit in hits]
    lower = jnp.concatenate(
        [jnp.where(row > target, 1.0, 0.0).astype(BF16) for target in targets], axis=1
    )
    first = dot(lower, jnp.ones((slots, slots_per), BF16))
    first_ref[...] = dot(jnp.ones((8, slots), BF16), lower, NT).astype(jnp.int32)
    place = pltpu.make_async_copy(first_ref, first_s, first_sem)
    place.start()
    sums = dot(jnp.concatenate(onehots, axis=0), before)
    taken = jnp.zeros((owners, slots_per), F32)
    named, packed_rows = [], []
    for s in range(subs):
        own = sums[s * owners : (s + 1) * owners]
        rank = jnp.sum(jnp.where(hits[s], own[:, :slots_per] + taken, 0.0), axis=0, keepdims=True)
        start = jnp.sum(jnp.where(hits[s], first, 0.0), axis=0, keepdims=True)
        taken = taken + own[:, slots_per:]
        rank = rank.astype(jnp.int32)
        dead = targets[s] == owners
        within = lax.rem(map_v[s : s + 1, :], 256) + 1
        named.append(jnp.where(id_place == rank, within, 0).astype(F32).astype(BF16))
        packed_rows.append(jnp.where(dead, -1, start.astype(jnp.int32) + rank))
        slot_ref[s : s + 1, :] = packed_rows[s]
    table = dot(jnp.concatenate(onehots, axis=1), jnp.concatenate(named, axis=1), NT)
    chunk = blocks * CAP + IDROWS
    sent = send_ref.reshape(owners * chunk, LANES)
    table_v[:owners, :] = table
    table_v[owners:, :] = jnp.zeros((8, LANES), F32)
    for o in range(owners):
        sent[o * chunk + blocks * CAP : (o + 1) * chunk, :] = table_v[o : o + IDROWS, :].astype(
            BF16
        )

    for copy in large:
        copy.wait()
    for s in range(subs):
        rest_v[:, s * slots_per : (s + 1) * slots_per] = dot(resid_v[s], basis_v[s]).astype(BF16)

    pick = jnp.where(
        iota((slots, slots), 0) == jnp.concatenate(packed_rows, axis=1), 1.0, 0.0
    ).astype(BF16)
    packed = dot(pick, rest_v[...], NT)
    for q in range(blocks):
        comp_v[q, :slots, :] = packed[:, q * LANES : (q + 1) * LANES]
        comp_v[q, slots:, :] = jnp.zeros((CAP, LANES), F32)
    place.wait()

    for o in range(owners):
        rows = pl.ds(first_s[0, o], CAP)
        for q in range(blocks):
            here = o * chunk + q * CAP
            sent[here : here + CAP, :] = comp_v[q, rows, :].astype(BF16)


def owner_kernel(recv_ref, inv_ref, back_ref, got_v, match_v):
    owners, _, rcols = back_ref.shape
    blocks = rcols // LANES
    cblock = inv_ref.shape[0]
    step = LANES // CAP
    chunk = blocks * CAP + IDROWS
    recv = recv_ref.reshape(owners * chunk, LANES)
    dof = iota((cblock, LANES), 0) + 1
    for t in range(owners // step):
        rows = slice(t * LANES, (t + 1) * LANES)
        named = jnp.zeros((IDROWS, LANES), BF16)
        for d in range(t * step, (t + 1) * step):
            named = named + recv[d * chunk + blocks * CAP : (d + 1) * chunk, :]
            for q in range(blocks):
                here = d * chunk + q * CAP
                got_v[d * CAP : (d + 1) * CAP, q * LANES : (q + 1) * LANES] = recv[
                    here : here + CAP, :
                ]
        named = named[0:1, :].astype(F32).astype(jnp.int32)
        match_v[:, rows] = jnp.where(dof == named, 1.0, 0.0).astype(BF16)
    total = dot(match_v[...], got_v[...])
    sol = dot(inv_ref[...], total.astype(BF16)).astype(BF16)
    part = dot(match_v[...], sol, TN).astype(BF16)
    back_ref[...] = part.reshape(owners, CAP, rcols)


def finish_kernel(
    back_ref, slot_ref, first_ref, resid_ref, inv_ref, basis_ref, out_hbm,
    first_s, comp_v, turned_v, out_v, first_sem, out_sem,
):
    subs, rcols, _ = resid_ref.shape
    slots_per = basis_ref.shape[2]
    slots = subs * slots_per
    owners = back_ref.shape[0]
    blocks = rcols // LANES
    place = pltpu.make_async_copy(first_ref, first_s, first_sem)
    place.start()
    comp_v[...] = jnp.zeros_like(comp_v)
    for s in range(subs):
        out_v[s] = dot(resid_ref[s], inv_ref[s], NT)
    place.wait()

    for o in range(owners):
        rows = pl.ds(first_s[0, o], CAP)
        for q in range(blocks):
            comp_v[q, rows, :] = back_ref[o, :, q * LANES : (q + 1) * LANES].astype(F32)
    for q in range(blocks):
        turned_v[q * LANES : (q + 1) * LANES, :] = comp_v[q, :slots, :].astype(BF16).T
    stores = []
    for first in range(0, subs, FINISH_BATCH):
        chosen = range(first, first + FINISH_BATCH)
        packed = jnp.concatenate([slot_ref[s : s + 1, :] for s in chosen], axis=1)
        pick = jnp.where(iota((slots, packed.shape[1]), 0) == packed, 1.0, 0.0).astype(BF16)
        pulled = dot(turned_v[...], pick).astype(BF16)
        for i, s in enumerate(chosen):
            out_v[s] = out_v[s] + dot(
                pulled[:, i * slots_per : (i + 1) * slots_per], basis_ref[s], NT
            )
            copy = pltpu.make_async_copy(out_v.at[s], out_hbm.at[s], out_sem.at[s])
            copy.start()
            stores.append(copy)
    for copy in stores:
        copy.wait()


ANY = pl.BlockSpec(memory_space=pl.ANY)
HBM = pl.BlockSpec(memory_space=pltpu.HBM)
INVMEM = pl.BlockSpec(memory_space=pltpu.VMEM)
INSMEM = pl.BlockSpec(memory_space=pltpu.SMEM)


def params(mib):
    return pltpu.CompilerParams(vmem_limit_bytes=mib * 1024 * 1024)


def pack(me, counts, cmap, resid, basis, owners):
    subs, rcols, _ = resid.shape
    slots_per = basis.shape[2]
    shape = (owners, (rcols // LANES * CAP + IDROWS) // IDROWS, IDROWS, LANES)
    return pl.pallas_call(
        pack_kernel,
        out_shape=(
            jax.ShapeDtypeStruct(shape, BF16),
            jax.ShapeDtypeStruct((subs, slots_per), jnp.int32),
            jax.ShapeDtypeStruct((8, owners), jnp.int32),
        ),
        in_specs=[INSMEM, HBM, HBM, HBM, HBM],
        out_specs=(INVMEM, INVMEM, INVMEM),
        scratch_shapes=[
            pltpu.SMEM(counts.shape, jnp.int32),
            pltpu.VMEM(cmap.shape, jnp.int32),
            pltpu.VMEM(resid.shape, BF16),
            pltpu.VMEM(basis.shape, BF16),
            pltpu.VMEM((rcols, subs * slots_per), BF16),
            pltpu.VMEM((rcols // LANES, subs * slots_per + CAP, LANES), F32),
            pltpu.VMEM((owners + 8, LANES), F32),
            pltpu.SMEM((8, owners), jnp.int32),
            pltpu.SemaphoreType.DMA((2,)),
            pltpu.SemaphoreType.DMA((2,)),
            pltpu.SemaphoreType.DMA,
        ],
        compiler_params=params(24),
        name="pack",
    )(me, *[pltpu.with_memory_space_constraint(x, pltpu.HBM) for x in (counts, cmap, resid, basis)])


def owner(recv, inv, rcols):
    owners = recv.shape[0]
    return pl.pallas_call(
        owner_kernel,
        out_shape=jax.ShapeDtypeStruct((owners, CAP, rcols), BF16),
        in_specs=[INVMEM, INVMEM],
        out_specs=INVMEM,
        scratch_shapes=[
            pltpu.VMEM((owners * CAP, rcols), BF16),
            pltpu.VMEM((inv.shape[0], owners * CAP), BF16),
        ],
        compiler_params=params(24),
        name="owner",
    )(recv, inv)


def finish(back, slot, first, resid, inv, basis):
    subs, rcols, _ = resid.shape
    slots = slot.size
    return pl.pallas_call(
        finish_kernel,
        out_shape=jax.ShapeDtypeStruct(resid.shape, F32),
        in_specs=[INVMEM] * 6,
        out_specs=ANY,
        scratch_shapes=[
            pltpu.SMEM(first.shape, jnp.int32),
            pltpu.VMEM((rcols // LANES, slots + CAP, LANES), F32),
            pltpu.VMEM((rcols, slots), BF16),
            pltpu.VMEM(resid.shape, F32),
            pltpu.SemaphoreType.DMA,
            pltpu.SemaphoreType.DMA((subs,)),
        ],
        compiler_params=params(32),
        name="finish",
    )(back, slot, first, resid, inv, basis)


def per_device(resid, local_inv, basis, coarse_inv, coarse_map, row_counts):
    owners = lax.axis_size("sub") * lax.axis_size("grp")
    me = lax.axis_index(AXES).astype(jnp.int32).reshape(1)
    send, slot, first = pack(me, row_counts, coarse_map, resid, basis, owners)
    recv = lax.all_to_all(send, AXES, split_axis=0, concat_axis=0, tiled=True)
    back = owner(recv, coarse_inv, resid.shape[1])
    back = lax.all_to_all(back, AXES, split_axis=0, concat_axis=0, tiled=True)
    return finish(back, slot, first, resid, local_inv, basis)


def solution(mesh):
    placed = (
        P(("sub", "grp"), None, None),
        P(("sub", "grp"), None, None),
        P(("sub", "grp"), None, None),
        P(("sub", "grp"), None),
        P(("sub", "grp"), None),
        P(("sub", "grp")),
    )
    return jax.shard_map(
        per_device,
        mesh=mesh,
        in_specs=placed,
        out_specs=P(("sub", "grp"), None, None),
        check_vma=False,
    )
```

time: 77.4 us -> 76.5 us (0.988)
  blocking collectives: 68.1 us -> 66.7 us
    all_to_all x1, blocking collectives: 39.3 us -> 37.9 us  [per_device(): recv = lax.all_to_all(send, AXES, split_axis=0, concat_axis=0, tiled=True)]
where the time goes in v5:
time: 76.5 us; the launch traced here: 76.3 us
  blocking collectives  66.7 us (87%)
  Pallas kernels  9.5 us (12%)
    all_to_all x1, blocking collectives, per_device(): recv = lax.all_to_all(send, AXES, split_axis=0, concat_axis=0, tiled=True)  37.9 us
    all_to_all x1, blocking collectives, per_device(): back = lax.all_to_all(back, AXES, split_axis=0, concat_axis=0, tiled=True)  28.8 us
    pallas_call x1, Pallas kernels, pack(): pl.pallas_call(pack_kernel, out_shape=(jax.ShapeDtypeStruct(shape, BF16),...  3.81 us
    pallas_call x1, Pallas kernels, finish(): pl.pallas_call(finish_kernel, out_shape=jax.ShapeDtypeStruct(resid.shape,...  3.6 us
    pallas_call x1, Pallas kernels, owner(): pl.pallas_call(owner_kernel, out_shape=jax.ShapeDtypeStruct((owners, CAP,...  2.09 us

profile of v5, /device:TPU:1, one launch (start us, length us, event | category | flops | bytes accessed | tf_op | source)
XLA Modules:
  0.0 76.3 jit_solution(14055052939457031706)
XLA Ops:
  0.0 3.8 %pack.1 = (bf16[128,13,4,128]{3,2,1,0:T(4,128)(2,1)S(1)}, s32[8,128]{1,0:T(8,128)S(1)}, s32[8,128]{1,0:T(8,128)S(1)}) custom-call(s32[1]{0:T(128)} %bitcast.me_ref, s32[8]{0:T(128)} %counts_hbm.1, s32[8,128]{1,0:T(8,128)} %map_hbm.1, bf16[8,384,256]{2,1,0:T(8,128)(2,1)} %resid_ref.1, bf16[8,256,128]{2,1,0:T(8,128)(2,1)} %basis_ref.1), custom_call_target="tpu_custom_call" | custom-call | tf_op jit(solution)/shard_map/pack/pallas_call | solution.py:193
  3.8 0.0 copy-start.3
  3.8 37.9 %all_to_all.10.recv_ref = bf16[128,13,4,128]{3,2,1,0:T(4,128)(2,1)S(1)} all-to-all(bf16[128,13,4,128]{3,2,1,0:T(4,128)(2,1)S(1)} %get-tuple-element.8), channel_id=1, replica_groups=mesh['sub'=32,'grp'=4] {'sub','grp'}, dimensions={0} | all-to-all | bytes 3407872 | tf_op jit(solution)/shard_map/all_to_all | solution.py:261
  41.8 0.0 copy-done.3
  41.8 2.1 %owner.1 = bf16[128,16,384]{2,1,0:T(8,128)(2,1)S(1)} custom-call(bf16[128,13,4,128]{3,2,1,0:T(4,128)(2,1)S(1)} %all_to_all.10.recv_ref, bf16[256,256]{1,0:T(8,128)(2,1)S(1)} %copy-done.3), custom_call_target="tpu_custom_call" | custom-call | tf_op jit(solution)/shard_map/owner/pallas_call | solution.py:222
  43.9 0.0 copy-start
  43.9 0.0 copy-start.1
  43.9 0.0 copy-start.2
  43.9 28.8 %all_to_all.11.back_ref = bf16[128,16,384]{2,1,0:T(8,128)(2,1)S(1)} all-to-all(bf16[128,16,384]{2,1,0:T(8,128)(2,1)S(1)} %owner.1), channel_id=1, replica_groups=mesh['sub'=32,'grp'=4] {'sub','grp'}, dimensions={0} | all-to-all | bytes 3145728 | tf_op jit(solution)/shard_map/all_to_all | solution.py:263
  72.7 0.0 copy-done
  72.7 0.0 copy-done.1
  72.7 0.0 copy-done.2
  72.7 3.6 %finish.1 = f32[8,384,256]{2,1,0:T(8,128)} custom-call(bf16[128,16,384]{2,1,0:T(8,128)(2,1)S(1)} %all_to_all.11.back_ref, s32[8,128]{1,0:T(8,128)S(1)} %get-tuple-element.9.slot_ref, s32[8,128]{1,0:T(8,128)S(1)} %get-tuple-element.10.first_ref, bf16[8,384,256]{2,1,0:T(8,128)(2,1)S(1)} %copy-done, bf16[8,256,256]{2,1,0:T(8,128)(2,1)S(1)} %copy-done.2, ...), custom_call_target="tpu_custom_call" | custom-call | tf_op jit(solution)/shard_map/finish/pallas_call | solution.py:239
Async XLA Ops:
  3.8 37.9 %copy-start.3 = (bf16[256,256]{1,0:T(8,128)(2,1)S(1)}, bf16[256,256]{1,0:T(8,128)(2,1)}, u32[]{:S(2)}) copy-start(bf16[256,256]{1,0:T(8,128)(2,1)} %inv_ref.2) | copy-start | bytes 393220
  43.9 28.8 %copy-start = (bf16[8,384,256]{2,1,0:T(8,128)(2,1)S(1)}, bf16[8,384,256]{2,1,0:T(8,128)(2,1)}, u32[]{:S(2)}) copy-start(bf16[8,384,256]{2,1,0:T(8,128)(2,1)} %resid_ref.1) | copy-start | bytes 4718596
  43.9 28.8 %copy-start.1 = (bf16[8,256,128]{2,1,0:T(8,128)(2,1)S(1)}, bf16[8,256,128]{2,1,0:T(8,128)(2,1)}, u32[]{:S(2)}) copy-start(bf16[8,256,128]{2,1,0:T(8,128)(2,1)} %basis_ref.1) | copy-start | bytes 1572868
  43.9 28.8 %copy-start.2 = (bf16[8,256,256]{2,1,0:T(8,128)(2,1)S(1)}, bf16[8,256,256]{2,1,0:T(8,128)(2,1)}, u32[]{:S(2)}) copy-start(bf16[8,256,256]{2,1,0:T(8,128)(2,1)} %inv_ref.3) | copy-start | bytes 3145732

commit v6 on v5

--- a/solution.py
+++ b/solution.py
@@ -25,7 +25,7 @@
 
 
 def pack_kernel(
-    me_ref, counts_hbm, map_hbm, resid_hbm, basis_hbm, send_ref, slot_ref, first_ref,
+    counts_hbm, map_hbm, resid_hbm, basis_hbm, send_ref, slot_ref, first_ref,
     counts_v, map_v, resid_v, basis_v, rest_v, comp_v, table_v, first_s, small_sem, in_sem, first_sem,
 ):
     subs, rcols, _ = resid_hbm.shape
@@ -51,9 +51,7 @@
     before = jnp.where(
         iota((slots_per, 2 * slots_per), 0) < iota((slots_per, 2 * slots_per), 1), 1.0, 0.0
     ).astype(BF16)
-    group = lax.rem(me_ref[0], LANES // CAP)
-    id_row = iota((LANES, slots_per), 0)
-    id_place = jnp.where(id_row // CAP == group, lax.rem(id_row, CAP), -1)
+    id_place = lax.rem(iota((LANES, slots_per), 0), CAP)
     targets = [
         jnp.where(lane < counts_v[s], map_v[s : s + 1, :] // 256, owners) for s in range(subs)
     ]
@@ -119,11 +117,13 @@
     chunk = blocks * CAP + IDROWS
     recv = recv_ref.reshape(owners * chunk, LANES)
     dof = iota((cblock, LANES), 0) + 1
+    part_of = iota((IDROWS, LANES), 1) // CAP
     for t in range(owners // step):
         rows = slice(t * LANES, (t + 1) * LANES)
         named = jnp.zeros((IDROWS, LANES), BF16)
         for d in range(t * step, (t + 1) * step):
-            named = named + recv[d * chunk + blocks * CAP : (d + 1) * chunk, :]
+            ids = recv[d * chunk + blocks * CAP : (d + 1) * chunk, :]
+            named = jnp.where(part_of == d % step, ids, named)
             for q in range(blocks):
                 here = d * chunk + q * CAP
                 got_v[d * CAP : (d + 1) * CAP, q * LANES : (q + 1) * LANES] = recv[
@@ -139,22 +139,20 @@
 
 def finish_kernel(
     back_ref, slot_ref, first_ref, resid_ref, inv_ref, basis_ref, out_hbm,
-    first_s, comp_v, turned_v, out_v, first_sem, out_sem,
+    comp_v, turned_v, out_v, out_sem,
 ):
     subs, rcols, _ = resid_ref.shape
     slots_per = basis_ref.shape[2]
     slots = subs * slots_per
     owners = back_ref.shape[0]
     blocks = rcols // LANES
-    place = pltpu.make_async_copy(first_ref, first_s, first_sem)
-    place.start()
+    starts = first_ref[0:1, :]
     comp_v[...] = jnp.zeros_like(comp_v)
     for s in range(subs):
         out_v[s] = dot(resid_ref[s], inv_ref[s], NT)
-    place.wait()
 
     for o in range(owners):
-        rows = pl.ds(first_s[0, o], CAP)
+        rows = pl.ds(starts[0, o], CAP)
         for q in range(blocks):
             comp_v[q, rows, :] = back_ref[o, :, q * LANES : (q + 1) * LANES].astype(F32)
     for q in range(blocks):
@@ -179,14 +177,13 @@
 ANY = pl.BlockSpec(memory_space=pl.ANY)
 HBM = pl.BlockSpec(memory_space=pltpu.HBM)
 INVMEM = pl.BlockSpec(memory_space=pltpu.VMEM)
-INSMEM = pl.BlockSpec(memory_space=pltpu.SMEM)
 
 
 def params(mib):
     return pltpu.CompilerParams(vmem_limit_bytes=mib * 1024 * 1024)
 
 
-def pack(me, counts, cmap, resid, basis, owners):
+def pack(counts, cmap, resid, basis, owners):
     subs, rcols, _ = resid.shape
     slots_per = basis.shape[2]
     shape = (owners, (rcols // LANES * CAP + IDROWS) // IDROWS, IDROWS, LANES)
@@ -197,7 +194,7 @@
             jax.ShapeDtypeStruct((subs, slots_per), jnp.int32),
             jax.ShapeDtypeStruct((8, owners), jnp.int32),
         ),
-        in_specs=[INSMEM, HBM, HBM, HBM, HBM],
+        in_specs=[HBM, HBM, HBM, HBM],
         out_specs=(INVMEM, INVMEM, INVMEM),
         scratch_shapes=[
             pltpu.SMEM(counts.shape, jnp.int32),
@@ -214,7 +211,7 @@
         ],
         compiler_params=params(24),
         name="pack",
-    )(me, *[pltpu.with_memory_space_constraint(x, pltpu.HBM) for x in (counts, cmap, resid, basis)])
+    )(*[pltpu.with_memory_space_constraint(x, pltpu.HBM) for x in (counts, cmap, resid, basis)])
 
 
 def owner(recv, inv, rcols):
@@ -242,11 +239,9 @@
         in_specs=[INVMEM] * 6,
         out_specs=ANY,
         scratch_shapes=[
-            pltpu.SMEM(first.shape, jnp.int32),
             pltpu.VMEM((rcols // LANES, slots + CAP, LANES), F32),
             pltpu.VMEM((rcols, slots), BF16),
             pltpu.VMEM(resid.shape, F32),
-            pltpu.SemaphoreType.DMA,
             pltpu.SemaphoreType.DMA((subs,)),
         ],
         compiler_params=params(32),
@@ -256,8 +251,7 @@
 
 def per_device(resid, local_inv, basis, coarse_inv, coarse_map, row_counts):
     owners = lax.axis_size("sub") * lax.axis_size("grp")
-    me = lax.axis_index(AXES).astype(jnp.int32).reshape(1)
-    send, slot, first = pack(me, row_counts, coarse_map, resid, basis, owners)
+    send, slot, first = pack(row_counts, coarse_map, resid, basis, owners)
     recv = lax.all_to_all(send, AXES, split_axis=0, concat_axis=0, tiled=True)
     back = owner(recv, coarse_inv, resid.shape[1])
     back = lax.all_to_all(back, AXES, split_axis=0, concat_axis=0, tiled=True)

time: 76.5 us -> 76.2 us (level)
  no operation moved by 1% of the time
where the time goes in v6:
time: 76.2 us; the launch traced here: 76.1 us
  blocking collectives  66.7 us (88%)
  Pallas kernels  9.28 us (12%)
    all_to_all x1, blocking collectives, per_device(): recv = lax.all_to_all(send, AXES, split_axis=0, concat_axis=0, tiled=True)  37.9 us
    all_to_all x1, blocking collectives, per_device(): back = lax.all_to_all(back, AXES, split_axis=0, concat_axis=0, tiled=True)  28.8 us
    pallas_call x1, Pallas kernels, pack(): pl.pallas_call(pack_kernel, out_shape=(jax.ShapeDtypeStruct(shape, BF16),...  3.81 us
    pallas_call x1, Pallas kernels, finish(): pl.pallas_call(finish_kernel, out_shape=jax.ShapeDtypeStruct(resid.shape,...  3.38 us
    pallas_call x1, Pallas kernels, owner(): pl.pallas_call(owner_kernel, out_shape=jax.ShapeDtypeStruct((owners, CAP,...  2.09 us

profile of v6, /device:TPU:1, one launch (start us, length us, event | category | flops | bytes accessed | tf_op | source)
XLA Modules:
  0.0 76.1 jit_solution(8436263576885311789)
XLA Ops:
  0.0 3.8 %pack.1 = (bf16[128,13,4,128]{3,2,1,0:T(4,128)(2,1)S(1)}, s32[8,128]{1,0:T(8,128)S(1)}, s32[8,128]{1,0:T(8,128)S(1)}) custom-call(s32[8]{0:T(128)} %counts_hbm.1, s32[8,128]{1,0:T(8,128)} %map_hbm.1, bf16[8,384,256]{2,1,0:T(8,128)(2,1)} %resid_ref.1, bf16[8,256,128]{2,1,0:T(8,128)(2,1)} %basis_ref.1), custom_call_target="tpu_custom_call" | custom-call | tf_op jit(solution)/shard_map/pack/pallas_call | solution.py:190
  3.8 0.0 copy-start.3
  3.8 37.9 %all_to_all.10.recv_ref = bf16[128,13,4,128]{3,2,1,0:T(4,128)(2,1)S(1)} all-to-all(bf16[128,13,4,128]{3,2,1,0:T(4,128)(2,1)S(1)} %get-tuple-element.8), channel_id=1, replica_groups=mesh['sub'=32,'grp'=4] {'sub','grp'}, dimensions={0} | all-to-all | bytes 3407872 | tf_op jit(solution)/shard_map/all_to_all | solution.py:255
  41.8 0.0 copy-done.3
  41.8 2.1 %owner.1 = bf16[128,16,384]{2,1,0:T(8,128)(2,1)S(1)} custom-call(bf16[128,13,4,128]{3,2,1,0:T(4,128)(2,1)S(1)} %all_to_all.10.recv_ref, bf16[256,256]{1,0:T(8,128)(2,1)S(1)} %copy-done.3), custom_call_target="tpu_custom_call" | custom-call | tf_op jit(solution)/shard_map/owner/pallas_call | solution.py:219
  43.9 0.0 copy-start
  43.9 0.0 copy-start.1
  43.9 0.0 copy-start.2
  43.9 28.8 %all_to_all.11.back_ref = bf16[128,16,384]{2,1,0:T(8,128)(2,1)S(1)} all-to-all(bf16[128,16,384]{2,1,0:T(8,128)(2,1)S(1)} %owner.1), channel_id=1, replica_groups=mesh['sub'=32,'grp'=4] {'sub','grp'}, dimensions={0} | all-to-all | bytes 3145728 | tf_op jit(solution)/shard_map/all_to_all | solution.py:257
  72.7 0.0 copy-done
  72.7 0.0 copy-done.1
  72.7 0.0 copy-done.2
  72.7 3.4 %finish.1 = f32[8,384,256]{2,1,0:T(8,128)} custom-call(bf16[128,16,384]{2,1,0:T(8,128)(2,1)S(1)} %all_to_all.11.back_ref, s32[8,128]{1,0:T(8,128)S(1)} %get-tuple-element.9.slot_ref, s32[8,128]{1,0:T(8,128)S(1)} %get-tuple-element.10.first_ref, bf16[8,384,256]{2,1,0:T(8,128)(2,1)S(1)} %copy-done, bf16[8,256,256]{2,1,0:T(8,128)(2,1)S(1)} %copy-done.2, ...), custom_call_target="tpu_custom_call" | custom-call | tf_op jit(solution)/shard_map/finish/pallas_call | solution.py:236
Async XLA Ops:
  3.8 37.9 %copy-start.3 = (bf16[256,256]{1,0:T(8,128)(2,1)S(1)}, bf16[256,256]{1,0:T(8,128)(2,1)}, u32[]{:S(2)}) copy-start(bf16[256,256]{1,0:T(8,128)(2,1)} %inv_ref.2) | copy-start | bytes 393220
  43.9 28.8 %copy-start = (bf16[8,384,256]{2,1,0:T(8,128)(2,1)S(1)}, bf16[8,384,256]{2,1,0:T(8,128)(2,1)}, u32[]{:S(2)}) copy-start(bf16[8,384,256]{2,1,0:T(8,128)(2,1)} %resid_ref.1) | copy-start | bytes 4718596
  43.9 28.8 %copy-start.1 = (bf16[8,256,128]{2,1,0:T(8,128)(2,1)S(1)}, bf16[8,256,128]{2,1,0:T(8,128)(2,1)}, u32[]{:S(2)}) copy-start(bf16[8,256,128]{2,1,0:T(8,128)(2,1)} %basis_ref.1) | copy-start | bytes 1572868
  43.9 28.8 %copy-start.2 = (bf16[8,256,256]{2,1,0:T(8,128)(2,1)S(1)}, bf16[8,256,256]{2,1,0:T(8,128)(2,1)}, u32[]{:S(2)}) copy-start(bf16[8,256,256]{2,1,0:T(8,128)(2,1)} %inv_ref.3) | copy-start | bytes 3145732

commit v7 on v6

--- a/solution.py
+++ b/solution.py
@@ -26,7 +26,7 @@
 
 def pack_kernel(
     counts_hbm, map_hbm, resid_hbm, basis_hbm, send_ref, slot_ref, first_ref,
-    counts_v, map_v, resid_v, basis_v, rest_v, comp_v, table_v, first_s, small_sem, in_sem, first_sem,
+    counts_v, map_v, resid_v, basis_v, rest_v, comp_v, table_v, small_sem, in_sem,
 ):
     subs, rcols, _ = resid_hbm.shape
     slots_per = basis_hbm.shape[2]
@@ -62,8 +62,6 @@
     )
     first = dot(lower, jnp.ones((slots, slots_per), BF16))
     first_ref[...] = dot(jnp.ones((8, slots), BF16), lower, NT).astype(jnp.int32)
-    place = pltpu.make_async_copy(first_ref, first_s, first_sem)
-    place.start()
     sums = dot(jnp.concatenate(onehots, axis=0), before)
     taken = jnp.zeros((owners, slots_per), F32)
     named, packed_rows = [], []
@@ -100,10 +98,10 @@
     for q in range(blocks):
         comp_v[q, :slots, :] = packed[:, q * LANES : (q + 1) * LANES]
         comp_v[q, slots:, :] = jnp.zeros((CAP, LANES), F32)
-    place.wait()
-
+
+    starts = first_ref[0:1, :]
     for o in range(owners):
-        rows = pl.ds(first_s[0, o], CAP)
+        rows = pl.ds(starts[0, o], CAP)
         for q in range(blocks):
             here = o * chunk + q * CAP
             sent[here : here + CAP, :] = comp_v[q, rows, :].astype(BF16)
@@ -204,10 +202,8 @@
             pltpu.VMEM((rcols, subs * slots_per), BF16),
             pltpu.VMEM((rcols // LANES, subs * slots_per + CAP, LANES), F32),
             pltpu.VMEM((owners + 8, LANES), F32),
-            pltpu.SMEM((8, owners), jnp.int32),
             pltpu.SemaphoreType.DMA((2,)),
             pltpu.SemaphoreType.DMA((2,)),
-            pltpu.SemaphoreType.DMA,
         ],
         compiler_params=params(24),
         name="pack",

time: 76.2 us -> 76.2 us (level)
  no operation moved by 1% of the time
where the time goes in v7:
time: 76.2 us; the launch traced here: 76 us
  blocking collectives  66.7 us (88%)
  Pallas kernels  9.25 us (12%)
    all_to_all x1, blocking collectives, per_device(): recv = lax.all_to_all(send, AXES, split_axis=0, concat_axis=0, tiled=True)  37.9 us
    all_to_all x1, blocking collectives, per_device(): back = lax.all_to_all(back, AXES, split_axis=0, concat_axis=0, tiled=True)  28.8 us
    pallas_call x1, Pallas kernels, pack(): pl.pallas_call(pack_kernel, out_shape=(jax.ShapeDtypeStruct(shape, BF16),...  3.79 us
    pallas_call x1, Pallas kernels, finish(): pl.pallas_call(finish_kernel, out_shape=jax.ShapeDtypeStruct(resid.shape,...  3.37 us
    pallas_call x1, Pallas kernels, owner(): pl.pallas_call(owner_kernel, out_shape=jax.ShapeDtypeStruct((owners, CAP,...  2.09 us

profile of v7, /device:TPU:1, one launch (start us, length us, event | category | flops | bytes accessed | tf_op | source)
XLA Modules:
  0.0 76.0 jit_solution(10687705411974254805)
XLA Ops:
  0.0 3.8 %pack.1 = (bf16[128,13,4,128]{3,2,1,0:T(4,128)(2,1)S(1)}, s32[8,128]{1,0:T(8,128)S(1)}, s32[8,128]{1,0:T(8,128)S(1)}) custom-call(s32[8]{0:T(128)} %counts_hbm.1, s32[8,128]{1,0:T(8,128)} %map_hbm.1, bf16[8,384,256]{2,1,0:T(8,128)(2,1)} %resid_ref.1, bf16[8,256,128]{2,1,0:T(8,128)(2,1)} %basis_ref.1), custom_call_target="tpu_custom_call" | custom-call | tf_op jit(solution)/shard_map/pack/pallas_call | solution.py:188
  3.8 0.0 copy-start.3
  3.8 37.9 %all_to_all.10.recv_ref = bf16[128,13,4,128]{3,2,1,0:T(4,128)(2,1)S(1)} all-to-all(bf16[128,13,4,128]{3,2,1,0:T(4,128)(2,1)S(1)} %get-tuple-element.8), channel_id=1, replica_groups=mesh['sub'=32,'grp'=4] {'sub','grp'}, dimensions={0} | all-to-all | bytes 3407872 | tf_op jit(solution)/shard_map/all_to_all | solution.py:251
  41.7 0.0 copy-done.3
  41.7 2.1 %owner.1 = bf16[128,16,384]{2,1,0:T(8,128)(2,1)S(1)} custom-call(bf16[128,13,4,128]{3,2,1,0:T(4,128)(2,1)S(1)} %all_to_all.10.recv_ref, bf16[256,256]{1,0:T(8,128)(2,1)S(1)} %copy-done.3), custom_call_target="tpu_custom_call" | custom-call | tf_op jit(solution)/shard_map/owner/pallas_call | solution.py:215
  43.8 0.0 copy-start
  43.8 0.0 copy-start.1
  43.9 0.0 copy-start.2
  43.9 28.8 %all_to_all.11.back_ref = bf16[128,16,384]{2,1,0:T(8,128)(2,1)S(1)} all-to-all(bf16[128,16,384]{2,1,0:T(8,128)(2,1)S(1)} %owner.1), channel_id=1, replica_groups=mesh['sub'=32,'grp'=4] {'sub','grp'}, dimensions={0} | all-to-all | bytes 3145728 | tf_op jit(solution)/shard_map/all_to_all | solution.py:253
  72.7 0.0 copy-done
  72.7 0.0 copy-done.1
  72.7 0.0 copy-done.2
  72.7 3.4 %finish.1 = f32[8,384,256]{2,1,0:T(8,128)} custom-call(bf16[128,16,384]{2,1,0:T(8,128)(2,1)S(1)} %all_to_all.11.back_ref, s32[8,128]{1,0:T(8,128)S(1)} %get-tuple-element.9.slot_ref, s32[8,128]{1,0:T(8,128)S(1)} %get-tuple-element.10.first_ref, bf16[8,384,256]{2,1,0:T(8,128)(2,1)S(1)} %copy-done, bf16[8,256,256]{2,1,0:T(8,128)(2,1)S(1)} %copy-done.2, ...), custom_call_target="tpu_custom_call" | custom-call | tf_op jit(solution)/shard_map/finish/pallas_call | solution.py:232
Async XLA Ops:
  3.8 37.9 %copy-start.3 = (bf16[256,256]{1,0:T(8,128)(2,1)S(1)}, bf16[256,256]{1,0:T(8,128)(2,1)}, u32[]{:S(2)}) copy-start(bf16[256,256]{1,0:T(8,128)(2,1)} %inv_ref.2) | copy-start | bytes 393220
  43.8 28.8 %copy-start = (bf16[8,384,256]{2,1,0:T(8,128)(2,1)S(1)}, bf16[8,384,256]{2,1,0:T(8,128)(2,1)}, u32[]{:S(2)}) copy-start(bf16[8,384,256]{2,1,0:T(8,128)(2,1)} %resid_ref.1) | copy-start | bytes 4718596
  43.8 28.8 %copy-start.1 = (bf16[8,256,128]{2,1,0:T(8,128)(2,1)S(1)}, bf16[8,256,128]{2,1,0:T(8,128)(2,1)}, u32[]{:S(2)}) copy-start(bf16[8,256,128]{2,1,0:T(8,128)(2,1)} %basis_ref.1) | copy-start | bytes 1572868
  43.9 28.8 %copy-start.2 = (bf16[8,256,256]{2,1,0:T(8,128)(2,1)S(1)}, bf16[8,256,256]{2,1,0:T(8,128)(2,1)}, u32[]{:S(2)}) copy-start(bf16[8,256,256]{2,1,0:T(8,128)(2,1)} %inv_ref.3) | copy-start | bytes 3145732

commit v8 on v7

--- a/solution.py
+++ b/solution.py
@@ -145,7 +145,8 @@
     owners = back_ref.shape[0]
     blocks = rcols // LANES
     starts = first_ref[0:1, :]
-    comp_v[...] = jnp.zeros_like(comp_v)
+    spare = comp_v.shape[1] - slots // 2
+    comp_v[:, slots // 2 :, :] = jnp.zeros((blocks, spare, LANES), F32)
     for s in range(subs):
         out_v[s] = dot(resid_ref[s], inv_ref[s], NT)
 

time: 76.2 us -> 76.2 us (level)
  no operation moved by 1% of the time
where the time goes in v8:
time: 76.2 us; the launch traced here: 76 us
  blocking collectives  66.7 us (88%)
  Pallas kernels  9.2 us (12%)
    all_to_all x1, blocking collectives, per_device(): recv = lax.all_to_all(send, AXES, split_axis=0, concat_axis=0, tiled=True)  37.9 us
    all_to_all x1, blocking collectives, per_device(): back = lax.all_to_all(back, AXES, split_axis=0, concat_axis=0, tiled=True)  28.8 us
    pallas_call x1, Pallas kernels, pack(): pl.pallas_call(pack_kernel, out_shape=(jax.ShapeDtypeStruct(shape, BF16),...  3.79 us
    pallas_call x1, Pallas kernels, finish(): pl.pallas_call(finish_kernel, out_shape=jax.ShapeDtypeStruct(resid.shape,...  3.32 us
    pallas_call x1, Pallas kernels, owner(): pl.pallas_call(owner_kernel, out_shape=jax.ShapeDtypeStruct((owners, CAP,...  2.09 us

profile of v8, /device:TPU:1, one launch (start us, length us, event | category | flops | bytes accessed | tf_op | source)
XLA Modules:
  0.0 76.0 jit_solution(10405893978265010625)
XLA Ops:
  0.0 3.8 %pack.1 = (bf16[128,13,4,128]{3,2,1,0:T(4,128)(2,1)S(1)}, s32[8,128]{1,0:T(8,128)S(1)}, s32[8,128]{1,0:T(8,128)S(1)}) custom-call(s32[8]{0:T(128)} %counts_hbm.1, s32[8,128]{1,0:T(8,128)} %map_hbm.1, bf16[8,384,256]{2,1,0:T(8,128)(2,1)} %resid_ref.1, bf16[8,256,128]{2,1,0:T(8,128)(2,1)} %basis_ref.1), custom_call_target="tpu_custom_call" | custom-call | tf_op jit(solution)/shard_map/pack/pallas_call | solution.py:189
  3.8 0.0 copy-start.3
  3.8 37.9 %all_to_all.10.recv_ref = bf16[128,13,4,128]{3,2,1,0:T(4,128)(2,1)S(1)} all-to-all(bf16[128,13,4,128]{3,2,1,0:T(4,128)(2,1)S(1)} %get-tuple-element.8), channel_id=1, replica_groups=mesh['sub'=32,'grp'=4] {'sub','grp'}, dimensions={0} | all-to-all | bytes 3407872 | tf_op jit(solution)/shard_map/all_to_all | solution.py:252
  41.7 0.0 copy-done.3
  41.7 2.1 %owner.1 = bf16[128,16,384]{2,1,0:T(8,128)(2,1)S(1)} custom-call(bf16[128,13,4,128]{3,2,1,0:T(4,128)(2,1)S(1)} %all_to_all.10.recv_ref, bf16[256,256]{1,0:T(8,128)(2,1)S(1)} %copy-done.3), custom_call_target="tpu_custom_call" | custom-call | tf_op jit(solution)/shard_map/owner/pallas_call | solution.py:216
  43.8 0.0 copy-start
  43.8 0.0 copy-start.1
  43.9 0.0 copy-start.2
  43.9 28.8 %all_to_all.11.back_ref = bf16[128,16,384]{2,1,0:T(8,128)(2,1)S(1)} all-to-all(bf16[128,16,384]{2,1,0:T(8,128)(2,1)S(1)} %owner.1), channel_id=1, replica_groups=mesh['sub'=32,'grp'=4] {'sub','grp'}, dimensions={0} | all-to-all | bytes 3145728 | tf_op jit(solution)/shard_map/all_to_all | solution.py:254
  72.7 0.0 copy-done
  72.7 0.0 copy-done.1
  72.7 0.0 copy-done.2
  72.7 3.3 %finish.1 = f32[8,384,256]{2,1,0:T(8,128)} custom-call(bf16[128,16,384]{2,1,0:T(8,128)(2,1)S(1)} %all_to_all.11.back_ref, s32[8,128]{1,0:T(8,128)S(1)} %get-tuple-element.9.slot_ref, s32[8,128]{1,0:T(8,128)S(1)} %get-tuple-element.10.first_ref, bf16[8,384,256]{2,1,0:T(8,128)(2,1)S(1)} %copy-done, bf16[8,256,256]{2,1,0:T(8,128)(2,1)S(1)} %copy-done.2, ...), custom_call_target="tpu_custom_call" | custom-call | tf_op jit(solution)/shard_map/finish/pallas_call | solution.py:233
Async XLA Ops:
  3.8 37.9 %copy-start.3 = (bf16[256,256]{1,0:T(8,128)(2,1)S(1)}, bf16[256,256]{1,0:T(8,128)(2,1)}, u32[]{:S(2)}) copy-start(bf16[256,256]{1,0:T(8,128)(2,1)} %inv_ref.2) | copy-start | bytes 393220
  43.8 28.8 %copy-start = (bf16[8,384,256]{2,1,0:T(8,128)(2,1)S(1)}, bf16[8,384,256]{2,1,0:T(8,128)(2,1)}, u32[]{:S(2)}) copy-start(bf16[8,384,256]{2,1,0:T(8,128)(2,1)} %resid_ref.1) | copy-start | bytes 4718596
  43.8 28.8 %copy-start.1 = (bf16[8,256,128]{2,1,0:T(8,128)(2,1)S(1)}, bf16[8,256,128]{2,1,0:T(8,128)(2,1)}, u32[]{:S(2)}) copy-start(bf16[8,256,128]{2,1,0:T(8,128)(2,1)} %basis_ref.1) | copy-start | bytes 1572868
  43.9 28.8 %copy-start.2 = (bf16[8,256,256]{2,1,0:T(8,128)(2,1)S(1)}, bf16[8,256,256]{2,1,0:T(8,128)(2,1)}, u32[]{:S(2)}) copy-start(bf16[8,256,256]{2,1,0:T(8,128)(2,1)} %inv_ref.3) | copy-start | bytes 3145732
